TPU v7x, 32 devices: a whole 2x2x4 slice. The times are simulated.
32 devices in a mesh: energy: 8 (over y, x, core), blk: 4 (over z).
Axes of the slice: x: 2, y: 2, z: 4, core: 2. Of those that a mesh axis runs over, the one named last changes fastest.
Arguments:
- lesser_green: bfloat16 [16, 4, 2, 384, 384], P('energy', 'blk'), may hold values from -4.1875 to 4.1875
- greater_green: bfloat16 [16, 4, 2, 384, 384], P('energy', 'blk'), may hold values from -4.1875 to 4.1875
- coulomb_blocks: bfloat16 [4, 3, 2, 384, 384], P('blk'), may hold values from -0.21875 to 0.21875
Outputs:
- lesser_sigma: bfloat16 [16, 4, 2, 384, 384], P('energy', 'blk')
- greater_sigma: bfloat16 [16, 4, 2, 384, 384], P('energy', 'blk')
All inputs are finite; a program needn't handle non-finite values.
Results may differ from a plain program's by a relative error of at most 0.017.
Values may be sent and summed in bfloat16 or wider, within the bound.
No kernel may reach another device: no remote copies, remote signals or barrier semaphores. Data moves between devices by JAX's collectives and lax.ppermute only.
A program may use at most 128 MiB of HBM per device.

v0:
```python
import functools
import math

import jax
import jax.numpy as jnp
from jax import lax
from jax.experimental import pallas as pl
from jax.experimental.pallas import tpu as pltpu
from jax.sharding import PartitionSpec as P

f32 = jnp.float32
bf16 = jnp.bfloat16


def swap(value, distance):
    count = lax.axis_size("energy")
    return lax.ppermute(value, "energy", [(i, i ^ distance) for i in range(count)])


def trade(value, first):
    count = lax.axis_size("blk")
    lows = range(first, count - 1, 2)
    return lax.ppermute(value, "blk", [(i, i + 1) for i in lows] + [(i + 1, i) for i in lows])


def row_block(rows):
    for size in (16, 8):
        if rows % size == 0:
            return size
    return rows


def out_like(shape):
    return jax.ShapeDtypeStruct(shape, bf16)


def vpu_cost(total, elements, moved):
    return pl.CostEstimate(
        flops=3 * total * (total + 1) * elements, bytes_accessed=2 * moved, transcendentals=0
    )


def tiles(rows, cols, body):
    lanes = 128 if cols % 128 == 0 else cols
    sub = 8 if rows % 8 == 0 else rows
    across = cols // lanes

    def step(t, carry):
        r = pl.multiple_of(lax.div(t, across) * sub, sub)
        c = pl.multiple_of(lax.rem(t, across) * lanes, lanes)
        body((pl.ds(r, sub), pl.ds(c, lanes)))
        return carry

    lax.fori_loop(0, (rows // sub) * across, step, 0)


def lag_of(total, slots, chunks, chunk, slot, i):
    return (chunks - 1 - chunk) * (total // chunks) + slot * (total // (chunks * slots)) + i


def load_greens(slots, inner, where, mine, sib, put):
    chip, core = where[0], where[1]
    for half, sources in ((core, mine), (1 - core, sib)):
        j = 0
        for source in sources:
            for k in range(source.shape[0]):
                for i in range(inner):
                    put((2 * (chip ^ j) + half) * inner + i, source, k, i)
                j += 1


def correlate_kernel(slots, inner, chunks, chunk, halves, extra, where, *rest):
    mine, sib = rest[:halves], rest[halves : 2 * halves][::-1]
    rest = rest[2 * halves + extra :]
    outs, (x_scr, y_scr, o_scr) = rest[:slots], rest[slots:]
    chip, core = where[0], where[1]
    total = 2 * inner * slots
    rows, cols = mine[0].shape[-2:]

    def put(e, source, k, i):
        a = source[k, i, core, 0].astype(f32)
        b = source[k, i, core, 1].astype(f32)
        x_scr[0, e], x_scr[1, e], x_scr[2, e] = a, b, a + b
        a = source[k, i, 1 - core, 0].astype(f32)
        b = source[k, i, 1 - core, 1].astype(f32)
        y_scr[0, e], y_scr[1, e], y_scr[2, e] = a, b, a - b

    load_greens(slots, inner, where, mine, sib, put)
    factor = -1.0 / math.sqrt(total)
    width = 4
    first_lag = lag_of(total, slots, chunks, chunk, 0, 0)
    last_lag = first_lag + total // chunks

    def body(at):
        for base in range(first_lag, last_lag, width):
            lags = range(base, min(base + width, last_lag))
            sums = {}
            window = {}
            for e in range(total - base):
                y = [y_scr[(p, e) + at] for p in range(3)]
                for w in lags:
                    if e + w >= total:
                        continue
                    if e + w not in window:
                        window[e + w] = [x_scr[(p, e + w) + at] for p in range(3)]
                    terms = [window[e + w][p] * y[p] for p in range(3)]
                    sums[w] = [s + t for s, t in zip(sums[w], terms)] if w in sums else terms
                window.pop(e + base, None)
            for w in lags:
                first, second, third = sums[w]
                o_scr[(w - first_lag, 0) + at] = factor * (first + second)
                o_scr[(w - first_lag, 1) + at] = factor * (third - first + second)

    tiles(rows, cols, body)
    each = 2 * inner // chunks
    for j in range(slots):
        for i in range(each):
            outs[j][i] = o_scr[(chip ^ j) * each + i].astype(bf16)


def correlate(where, mine, sib, chunks, chunk, after):
    _, inner, _, _, rows, cols = mine[0].shape
    slots = sum(piece.shape[0] for piece in mine)
    total = 2 * inner * slots
    each = 2 * inner // chunks
    block = row_block(rows)
    in_specs = [
        pl.BlockSpec((piece.shape[0], inner, 2, 2, block, cols), lambda r, s: (0, 0, 0, 0, r, 0))
        for piece in (*mine, *sib[::-1])
    ]
    out_spec = pl.BlockSpec((each, 2, block, cols), lambda r, s: (0, 0, r, 0))
    return pl.pallas_call(
        functools.partial(correlate_kernel, slots, inner, chunks, chunk, len(mine), len(after)),
        name="correlate",
        out_shape=[out_like((each, 2, rows, cols))] * slots,
        grid_spec=pltpu.PrefetchScalarGridSpec(
            num_scalar_prefetch=1,
            grid=(rows // block,),
            in_specs=in_specs + [pl.BlockSpec(memory_space=pl.ANY)] * len(after),
            out_specs=[out_spec] * slots,
            scratch_shapes=[
                pltpu.VMEM((3, total, block, cols), f32),
                pltpu.VMEM((3, total, block, cols), f32),
                pltpu.VMEM((total // chunks, 2, block, cols), f32),
            ],
        ),
        compiler_params=pltpu.CompilerParams(vmem_limit_bytes=32 * 2**20),
        cost_estimate=vpu_cost(total, rows * cols // chunks, 4 * total * rows * cols),
    )(where, *mine, *sib[::-1], *after)


def sigma_kernel(slots, inner, chunks, halves, where, *rest):
    mine, sib = rest[:halves], rest[halves : 2 * halves][::-1]
    rest = rest[2 * halves :]
    screens = rest[: slots * chunks]
    outs = rest[slots * chunks : slots * chunks + slots]
    x_scr, y_scr, o_scr = rest[slots * chunks + slots :]
    chip, core = where[0], where[1]
    total = 2 * inner * slots
    rows, cols = mine[0].shape[-2:]
    each = 2 * inner // chunks

    def put(e, source, k, i):
        a = source[k, i, 0, 0].astype(f32)
        b = source[k, i, 0, 1].astype(f32)
        x_scr[0, e], x_scr[1, e], x_scr[2, e] = a, b, a + b

    load_greens(slots, inner, where, mine, sib, put)
    for j in range(slots):
        for chunk in range(chunks):
            source = screens[chunk * slots + j]
            for i in range(each):
                w = lag_of(total, slots, chunks, chunk, chip ^ j, i)
                a = source[i, 0].astype(f32)
                b = source[i, 1].astype(f32)
                y_scr[0, w], y_scr[1, w], y_scr[2, w] = a, b, a + b
    factor = 1.0 / math.sqrt(total)
    width = 4

    def body(at):
        for base in range(0, total, width):
            energies = range(base, min(base + width, total))
            sums = {}
            window = {}
            for w in range(min(base + width, total)):
                y = [y_scr[(p, w) + at] for p in range(3)]
                for e in energies:
                    if e < w:
                        continue
                    if e - w not in window:
                        window[e - w] = [x_scr[(p, e - w) + at] for p in range(3)]
                    terms = [window[e - w][p] * y[p] for p in range(3)]
                    sums[e] = [s + t for s, t in zip(sums[e], terms)] if e in sums else terms
                window.pop(base + width - 1 - w, None)
            for e in energies:
                first, second, third = sums[e]
                o_scr[(e, 0) + at] = factor * (first - second)
                o_scr[(e, 1) + at] = factor * (third - first - second)

    tiles(rows, cols, body)
    for j in range(slots):
        for side in range(2):
            half = core if side == 0 else 1 - core
            for i in range(inner):
                e = (2 * (chip ^ j) + half) * inner + i
                outs[j][side, i] = o_scr[e].astype(bf16)


def self_energy(where, mine, sib, screens, part, rows):
    _, inner, _, _, _, cols = mine[0].shape
    slots = sum(piece.shape[0] for piece in mine)
    chunks = len(screens)
    flat = [piece for chunk in screens for piece in chunk]
    each = flat[0].shape[0]
    total = 2 * inner * slots
    block = row_block(rows)
    steps = rows // block
    green_specs = [
        pl.BlockSpec(
            (piece.shape[0], inner, 1, 2, block, cols),
            lambda r, s: (0, 0, s[1], 0, part * steps + r, 0),
        )
        for piece in (*mine, *sib[::-1])
    ]
    screen_spec = pl.BlockSpec((each, 2, block, cols), lambda r, s: (0, 0, part * steps + r, 0))
    out_spec = pl.BlockSpec((2, inner, 2, block, cols), lambda r, s: (0, 0, 0, r, 0))
    return pl.pallas_call(
        functools.partial(sigma_kernel, slots, inner, chunks, len(mine)),
        name="sigma",
        out_shape=[out_like((2, inner, 2, rows, cols))] * slots,
        grid_spec=pltpu.PrefetchScalarGridSpec(
            num_scalar_prefetch=1,
            grid=(steps,),
            in_specs=green_specs + [screen_spec] * len(flat),
            out_specs=[out_spec] * slots,
            scratch_shapes=[
                pltpu.VMEM((3, total, block, cols), f32),
                pltpu.VMEM((3, total, block, cols), f32),
                pltpu.VMEM((total, 2, block, cols), f32),
            ],
        ),
        compiler_params=pltpu.CompilerParams(vmem_limit_bytes=32 * 2**20),
        cost_estimate=vpu_cost(total, rows * cols, 6 * total * rows * cols),
    )(where, *mine, *sib[::-1], *flat)


def cut_kernel(count, where, *rest):
    for k in range(count):
        for kind in range(2):
            rest[2 * count + k][0, kind] = rest[kind * count + k][0, 0]


def cut(where, greens, slots, wanted):
    inner, _, _, m, _ = greens[0].shape
    group = m // slots
    count = len(wanted)
    if group % 16:
        return [
            jnp.stack(
                [
                    lax.dynamic_slice_in_dim(g[:, 0], (where[0] ^ j) * group, group, axis=2)
                    for g in greens
                ],
                axis=1,
            )
            for j in wanted
        ]

    def block(j):
        return pl.BlockSpec((1, 1, 2, group, m), lambda e, s: (e, 0, 0, s[0] ^ j, 0))

    return pl.pallas_call(
        functools.partial(cut_kernel, count),
        name="cut_rows",
        out_shape=[out_like((inner, 2, 2, group, m))] * count,
        grid_spec=pltpu.PrefetchScalarGridSpec(
            num_scalar_prefetch=1,
            grid=(inner,),
            in_specs=[block(j) for j in wanted] * 2,
            out_specs=[pl.BlockSpec((1, 2, 2, group, m), lambda e, s: (e, 0, 0, 0, 0))] * count,
        ),
        compiler_params=pltpu.CompilerParams(vmem_limit_bytes=56 * 2**20),
        cost_estimate=pl.CostEstimate(flops=0, bytes_accessed=16 * inner * count * group * m, transcendentals=0),
    )(where, *([greens[0]] * count), *([greens[1]] * count))


def matrices_kernel(slots, where, coupling, left, right, *held):
    count, _, m, _ = coupling.shape
    group = m // slots
    chip = where[0]
    for o in range(count):
        real, imag = coupling[o, 0].astype(f32), coupling[o, 1].astype(f32)
        real_t, imag_t = real.T.astype(bf16), imag.T.astype(bf16)
        right[o, :m, :m] = real_t
        right[o, :m, m:] = -imag_t
        right[o, m:, :m] = imag_t
        right[o, m:, m:] = real_t
        if held:
            held[0][0], held[0][1] = real, imag
            source = held[0]
        else:
            source = coupling.at[o]
        for j in range(slots):
            start = pl.multiple_of((chip ^ j) * group, group)
            real = source[0, pl.ds(start, group), :].astype(bf16)
            imag = source[1, pl.ds(start, group), :].astype(bf16)
            low = j * group
            left[o, low : low + group, :m] = real
            left[o, low : low + group, m:] = -imag
            left[o, m + low : m + low + group, :m] = imag
            left[o, m + low : m + low + group, m:] = real


def coupling_matrices(where, coulomb, slots):
    count, _, m, _ = coulomb.shape
    vmem = pl.BlockSpec(memory_space=pltpu.VMEM)
    held = [] if (m // slots) % 16 == 0 else [pltpu.VMEM((2, m, m), f32)]
    return pl.pallas_call(
        functools.partial(matrices_kernel, slots),
        name="coupling",
        out_shape=[out_like((count, 2 * m, 2 * m))] * 2,
        in_specs=[pl.BlockSpec(memory_space=pltpu.SMEM), vmem],
        out_specs=[vmem, vmem],
        scratch_shapes=held,
        compiler_params=pltpu.CompilerParams(vmem_limit_bytes=24 * 2**20),
        cost_estimate=pl.CostEstimate(flops=0, bytes_accessed=20 * coulomb.size, transcendentals=0),
    )(where, coulomb)


def pack_kernel(pieces, extra, *refs):
    for k in range(pieces):
        refs[pieces + extra][k] = refs[k][...]


def pack(pieces, block=None, index=None, after=()):
    count = len(pieces)
    block = block or pieces[0].shape
    index = index or (0,) * len(block)
    size = math.prod(block)
    return pl.pallas_call(
        functools.partial(pack_kernel, count, len(after)),
        name="pack",
        out_shape=out_like((count,) + block),
        grid=(1,),
        in_specs=[pl.BlockSpec(block, lambda i: index)] * count
        + [pl.BlockSpec(memory_space=pl.ANY)] * len(after),
        out_specs=pl.BlockSpec((count,) + block, lambda i: (0,) * (1 + len(block))),
        compiler_params=pltpu.CompilerParams(vmem_limit_bytes=16 * 2**20),
        cost_estimate=pl.CostEstimate(flops=0, bytes_accessed=4 * count * size, transcendentals=0),
    )(*pieces, *after)


def screen_kernel(slots, each, final, where, left_ref, right_ref, *rest):
    odd = where[2]
    neighbours = (2 - 2 * odd, 2 * odd) if final else (1,)
    count = len(neighbours)
    per_source = 2 if final else slots
    sources, rest = rest[: per_source * count], rest[per_source * count :]
    if final:
        start_ref, rest = rest[0], rest[1:]
    outs, (pol, left) = rest[:-2], rest[-2:]
    rows, m = sources[0].shape[2:]
    chip = where[0]
    for n in range(count):
        near, far = sources[per_source * n], sources[per_source * n + 1 : per_source * (n + 1)]
        for j in range(slots):
            for part in range(2):
                start = pl.multiple_of(part * m + (chip ^ j) * rows, rows)
                for i in range(each):
                    if j == 0:
                        piece = near[i, part]
                    else:
                        piece = far[0][j - 1, i, part] if final else far[j - 1][i, part]
                    pol[n, i, pl.ds(start, rows), :] = piece.astype(pol.dtype)
    for n, o in enumerate(neighbours):
        both = jnp.concatenate([pol[n, i].astype(bf16) for i in range(each)], axis=1)
        product = jnp.dot(left_ref[o], both, preferred_element_type=f32).astype(bf16)
        for i in range(each):
            for part in range(2):
                left[i, :, (2 * n + part) * m : (2 * n + part + 1) * m] = product[
                    part * m : (part + 1) * m, i * m : (i + 1) * m
                ]
    for i in range(each):
        result = start_ref[i] if final else None
        for n, o in enumerate(neighbours):
            term = jnp.dot(
                left[i, :, 2 * n * m : 2 * (n + 1) * m],
                right_ref[o],
                preferred_element_type=f32,
            )
            result = term if result is None else result + term
        if not final:
            outs[0][i] = result
            continue
        result = result.astype(bf16)
        for j in range(slots):
            for part in range(2):
                outs[j][i, part] = result[j * rows : (j + 1) * rows, part * m : (part + 1) * m]


def screen(where, left_matrix, right_matrix, sources, slots, start=None):
    each, _, rows, m = sources[0].shape
    count = 1 if start is None else 2
    vmem = pl.BlockSpec(memory_space=pltpu.VMEM)
    flops = 16 * each * count * m * m * m
    moved = 4 * each * m * m * (count + 1) + 2 * (left_matrix.size + right_matrix.size)
    hold = bf16 if rows % 16 == 0 else f32
    final = start is not None
    if final:
        shapes = [out_like((each, 2, rows, m))] * slots
    else:
        shapes = [jax.ShapeDtypeStruct((each, m, 2 * m), f32)]
    operands = list(sources) + ([start] if final else [])
    found = pl.pallas_call(
        functools.partial(screen_kernel, slots, each, final),
        name="screen",
        out_shape=shapes,
        in_specs=[pl.BlockSpec(memory_space=pltpu.SMEM)] + [vmem] * (2 + len(operands)),
        out_specs=[vmem] * len(shapes),
        scratch_shapes=[
            pltpu.VMEM((count, each, 2 * m, m), hold),
            pltpu.VMEM((each, m, 2 * count * m), bf16),
        ],
        compiler_params=pltpu.CompilerParams(vmem_limit_bytes=44 * 2**20),
        cost_estimate=pl.CostEstimate(flops=flops, bytes_accessed=moved, transcendentals=0),
    )(where, left_matrix, right_matrix, *operands)
    return found if final else found[0]


def collect_kernel(slots, parts, where, *rest):
    count = slots * parts
    own, other = rest[:count], rest[count : count + parts]
    less, great = rest[count + parts :]
    core = where[1]
    for k in range(count):

        @pl.when(pl.program_id(0) == k)
        def _(k=k):
            h, j = divmod(k, slots)
            mine, theirs = own[k][0], other[h][j]
            less[:, 0] = jnp.where(core == 0, mine, theirs)
            great[:, 0] = jnp.where(core == 0, theirs, mine)


def collect(where, own, other, inner, m):
    parts, slots = len(own), len(own[0])
    rows = m // (slots * parts)
    if rows % 16:
        target = jnp.zeros((2, inner, 1, 2, m, m), bf16)
        for h in range(parts):
            for j in range(slots):
                pair = jnp.stack([own[h][j][0], other[h][j]])
                pair = jnp.where(where[1] == 0, pair, pair[::-1])[:, :, None]
                start = ((where[0] ^ j) * parts + h) * rows
                target = lax.dynamic_update_slice_in_dim(target, pair, start, axis=4)
        return target[0], target[1]
    flat = [piece for pieces in own for piece in pieces]
    vmem = [
        pl.BlockSpec((1, inner, 2, rows, m), lambda i, s: (0, 0, 0, 0, 0)) for _ in flat
    ] + [pl.BlockSpec((slots, inner, 2, rows, m), lambda i, s: (0, 0, 0, 0, 0)) for _ in other]
    shape = (inner, 1, 2, m, m)
    target = pl.BlockSpec(
        (inner, 1, 2, rows, m),
        lambda i, s: (0, 0, 0, (s[0] ^ lax.rem(i, slots)) * parts + lax.div(i, slots), 0),
    )
    return pl.pallas_call(
        functools.partial(collect_kernel, slots, parts),
        name="collect",
        out_shape=[out_like(shape)] * 2,
        grid_spec=pltpu.PrefetchScalarGridSpec(
            num_scalar_prefetch=1,
            grid=(parts * slots,),
            in_specs=vmem,
            out_specs=[target] * 2,
        ),
        compiler_params=pltpu.CompilerParams(vmem_limit_bytes=24 * 2**20),
        cost_estimate=pl.CostEstimate(
            flops=0, bytes_accessed=16 * inner * m * m, transcendentals=0
        ),
    )(where, *flat, *other)


def local(lesser_green, greater_green, coulomb_blocks):
    pieces = lax.axis_size("energy")
    slots = pieces // 2
    inner, _, _, m, _ = lesser_green.shape
    group = m // slots
    parts = 2 if group % 32 == 0 else 1
    rows = group // parts
    chunks = 2
    index = lax.axis_index("energy")
    where = jnp.stack([index // 2, index % 2, lax.axis_index("blk") % 2]).astype(jnp.int32)
    others = range(1, slots)

    both = (lesser_green, greater_green)
    found = cut(where, both, slots, list(others))
    greens = [swap(found[j - 1], 2 * j) for j in others]
    greens = [*cut(where, both, slots, [0]), *greens]
    left, right = coupling_matrices(where, coulomb_blocks[0], slots)

    middle = (slots + 1) // 2
    mine = [pack(group) for group in (greens[:middle], greens[middle:])]
    sib = [swap(piece, 1) for piece in mine]

    pol, near, after = [], [], []
    for c in range(chunks):
        found = correlate(where, mine, sib, chunks, c, after)
        after = [found[0]]
        pol.append([swap(found[j], 2 * j) for j in others])
        near.append([trade(found[0], 0), found[0], trade(found[0], 1)])

    starts = [screen(where, left, right, [near[c][1], *pol[c]], slots) for c in range(chunks)]

    screens = []
    after = [piece for triple in near for piece in (triple[0], triple[2])] + [near[-1][1]]
    for c in range(chunks):
        far = pack(pol[c], after=after)
        crossed = [near[c][0], trade(far, 0), near[c][2], trade(far, 1)]
        after = crossed[1::2] + starts
        found = screen(where, left, right, crossed, slots, starts[c])
        screens.append([found[0]] + [swap(found[j], 2 * j) for j in others])

    own, other = [], []
    for h in range(parts):
        found = self_energy(where, mine, sib, screens, h, rows)
        own.append([found[0]] + [swap(found[j], 2 * j) for j in others])
        other.append(swap(jnp.stack([piece[1] for piece in own[h]]), 1))
    return tuple(collect(where, own, other, inner, m))


def solution(mesh):
    return jax.shard_map(
        local,
        mesh=mesh,
        in_specs=(
            P("energy", "blk", None, None, None),
            P("energy", "blk", None, None, None),
            P("blk", None, None, None, None),
        ),
        out_specs=(P("energy", "blk", None, None, None), P("energy", "blk", None, None, None)),
        check_vma=False,
    )
```

profile of v0, /device:TPU:0, one launch (start us, length us, event | category | flops | bytes accessed | tf_op | source)
XLA Modules:
  0.0 163.6 jit_solution(6613904582309095398)
XLA Ops:
  1.2 3.2 %cut_rows.3 = (bf16[2,2,2,96,384]{4,3,2,1,0:T(8,128)(2,1)}, bf16[2,2,2,96,384]{4,3,2,1,0:T(8,128)(2,1)}, bf16[2,2,2,96,384]{4,3,2,1,0:T(8,128)(2,1)}) custom-call(s32[3]{0:T(128)} %pad_add_fusion.where, bf16[2,1,2,384,384]{4,3,2,1,0:T(8,128)(2,1)} %rest_2_.1, bf16[2,1,2,384,384]{4,3,2,1,0:T(8,128)(2,1)} %rest_2_.1, bf16[2,1,2,384,384]{4,3,2,1,0:T(8,128)(2,1)} %rest_2_.1, ...), custom_call_target="tpu_custom_call" | custom-call | bytes 3538944 | tf_op jit(solution)/shard_map/cut_rows/pallas_call | solution.py:272
  4.5 3.0 %collective-permute-start.1 = (bf16[2,2,2,96,384]{4,3,2,1,0:T(8,128)(2,1)}, bf16[2,2,2,96,384]{4,3,2,1,0:T(8,128)(2,1)S(1)}, u32[]{:S(2)}, u32[]{:S(2)}) collective-permute-start(bf16[2,2,2,96,384]{4,3,2,1,0:T(8,128)(2,1)} %get-tuple-element.32), channel_id=1, source_target_pairs={{0,16},{4,20},{8,24},{12,28},{16,0},{20,4},{24,8},{28,12},{1,17},{... | collective-permute-start | bytes 1769480 | tf_op jit(solution)/shard_map/ppermute | solution.py:17
  7.4 1.4 collective-permute-start.2
  9.0 2.6 %cut_rows.2.refs_0_ = bf16[2,2,2,96,384]{4,3,2,1,0:T(8,128)(2,1)} custom-call(s32[3]{0:T(128)} %pad_add_fusion.where, bf16[2,1,2,384,384]{4,3,2,1,0:T(8,128)(2,1)} %rest_2_.1, bf16[2,1,2,384,384]{4,3,2,1,0:T(8,128)(2,1)} %rest_5_.1), custom_call_target="tpu_custom_call" | custom-call | bytes 1179648 | tf_op jit(solution)/shard_map/cut_rows/pallas_call | solution.py:272
  11.5 22.1 %collective-permute-done.1.refs_0_ = bf16[2,2,2,96,384]{4,3,2,1,0:T(8,128)(2,1)S(1)} collective-permute-done((bf16[2,2,2,96,384]{4,3,2,1,0:T(8,128)(2,1)}, bf16[2,2,2,96,384]{4,3,2,1,0:T(8,128)(2,1)S(1)}, u32[]{:S(2)}, u32[]{:S(2)}) %collective-permute-start.1) | collective-permute-done | bytes 589856 | tf_op jit(solution)/shard_map/ppermute | solution.py:17
  33.8 1.1 collective-permute-done.refs_1_
  35.1 1.6 collective-permute-done.3.rest_2_
  36.6 1.7 %collective-permute-done.4.rest_3_ = bf16[2,2,2,2,96,384]{5,4,3,2,1,0:T(8,128)(2,1)S(1)} collective-permute-done((bf16[2,2,2,2,96,384]{5,4,3,2,1,0:T(8,128)(2,1)S(1)}, bf16[2,2,2,2,96,384]{5,4,3,2,1,0:T(8,128)(2,1)S(1)}, u32[]{:S(2)}, u32[]{:S(2)}) %collective-permute-start.4) | collective-permute-done | bytes 1179680 | tf_op jit(solution)/shard_map/ppermute | solution.py:17
  38.3 4.2 %correlate.2 = (bf16[2,2,96,384]{3,2,1,0:T(8,128)(2,1)S(1)}, bf16[2,2,96,384]{3,2,1,0:T(8,128)(2,1)S(1)}, bf16[2,2,96,384]{3,2,1,0:T(8,128)(2,1)S(1)}, bf16[2,2,96,384]{3,2,1,0:T(8,128)(2,1)S(1)}) custom-call(s32[3]{0:T(128)S(1)} %copy-done.3, bf16[2,2,2,2,96,384]{5,4,3,2,1,0:T(8,128)(2,1)S(1)} %pack.4.rest_0_, ...), custom_call_target="tpu_custom_call" | custom-call | flops 15040512 | bytes 4718592 | tf_op jit(solution)/shard_map/correlate/pallas_call | solution.py:132
  42.5 1.8 %collective-permute-start.6 = (bf16[2,2,96,384]{3,2,1,0:T(8,128)(2,1)S(1)}, bf16[2,2,96,384]{3,2,1,0:T(8,128)(2,1)S(1)}, u32[]{:S(2)}, u32[]{:S(2)}) collective-permute-start(bf16[2,2,96,384]{3,2,1,0:T(8,128)(2,1)S(1)} %get-tuple-element.37), channel_id=1, source_target_pairs={{0,8},{4,12},{8,0},{12,4},{16,24},{20,28},{24,16},{28,20},{1,9},{5... | collective-permute-start | bytes 884744 | tf_op jit(solution)/shard_map/ppermute | solution.py:17
  44.3 1.5 collective-permute-start.7
  46.5 4.4 %collective-permute-start.5 = (bf16[2,2,96,384]{3,2,1,0:T(8,128)(2,1)S(1)}, bf16[2,2,96,384]{3,2,1,0:T(8,128)(2,1)S(1)}, u32[]{:S(2)}, u32[]{:S(2)}) collective-permute-start(bf16[2,2,96,384]{3,2,1,0:T(8,128)(2,1)S(1)} %get-tuple-element.36.rest_4_.rest_0_), channel_id=1, source_target_pairs={{0,1},{2,3},{1,0},{3,2},{4,5},{6,7},{5,4},{7,6},{8,9},{10,11},{9,8... | collective-permute-start | bytes 884744 | tf_op jit(solution)/shard_map/ppermute | solution.py:23
  51.4 6.3 %correlate.3 = (bf16[2,2,96,384]{3,2,1,0:T(8,128)(2,1)S(1)}, bf16[2,2,96,384]{3,2,1,0:T(8,128)(2,1)S(1)}, bf16[2,2,96,384]{3,2,1,0:T(8,128)(2,1)S(1)}, bf16[2,2,96,384]{3,2,1,0:T(8,128)(2,1)S(1)}) custom-call(s32[3]{0:T(128)S(1)} %copy-done.3, bf16[2,2,2,2,96,384]{5,4,3,2,1,0:T(8,128)(2,1)S(1)} %pack.4.rest_0_, ...), custom_call_target="tpu_custom_call" | custom-call | flops 15040512 | bytes 4718592 | tf_op jit(solution)/shard_map/correlate/pallas_call | solution.py:132
  58.6 2.4 %collective-permute-start.10 = (bf16[2,2,96,384]{3,2,1,0:T(8,128)(2,1)S(1)}, bf16[2,2,96,384]{3,2,1,0:T(8,128)(2,1)S(1)}, u32[]{:S(2)}, u32[]{:S(2)}) collective-permute-start(bf16[2,2,96,384]{3,2,1,0:T(8,128)(2,1)S(1)} %get-tuple-element.40.refs_7_.rest_0_), channel_id=1, source_target_pairs={{0,1},{2,3},{1,0},{3,2},{4,5},{6,7},{5,4},{7,6},{8,9},{10,11},{9,8... | collective-permute-start | bytes 884744 | tf_op jit(solution)/shard_map/ppermute | solution.py:23
  61.0 5.3 %collective-permute-done.10.refs_5_.rest_0_ = bf16[2,2,96,384]{3,2,1,0:T(8,128)(2,1)S(1)} collective-permute-done((bf16[2,2,96,384]{3,2,1,0:T(8,128)(2,1)S(1)}, bf16[2,2,96,384]{3,2,1,0:T(8,128)(2,1)S(1)}, u32[]{:S(2)}, u32[]{:S(2)}) %collective-permute-start.10) | collective-permute-done | bytes 294944 | tf_op jit(solution)/shard_map/ppermute | solution.py:23
  67.1 4.6 %collective-permute-start.12 = (bf16[3,2,2,96,384]{4,3,2,1,0:T(8,128)(2,1)S(1)}, bf16[3,2,2,96,384]{4,3,2,1,0:T(8,128)(2,1)S(1)}, u32[]{:S(2)}, u32[]{:S(2)}) collective-permute-start(bf16[3,2,2,96,384]{4,3,2,1,0:T(8,128)(2,1)S(1)} %pack.6), channel_id=1, source_target_pairs={{0,1},{2,3},{1,0},{3,2},{4,5},{6,7},{5,4},{7,6},{8,9},{10,11},{9,8... | collective-permute-start | bytes 2654216 | tf_op jit(solution)/shard_map/ppermute | solution.py:23
  71.7 1.5 collective-permute-start.17
  73.2 1.5 collective-permute-start.18
  75.5 1.4 coupling.1
  76.9 1.7 %copy-done = bf16[3,768,768]{2,1,0:T(8,128)(2,1)} copy-done((bf16[3,768,768]{2,1,0:T(8,128)(2,1)}, bf16[3,768,768]{2,1,0:T(8,128)(2,1)S(1)}, u32[]{:S(2)}) %copy-start) | copy-done | bytes 3538968
  78.7 4.1 %screen.4.rest_4_.refs_5_ = f32[2,384,768]{2,1,0:T(8,128)S(1)} custom-call(s32[3]{0:T(128)S(1)} %copy-done.3, bf16[3,768,768]{2,1,0:T(8,128)(2,1)S(1)} %get-tuple-element.34.left_ref, bf16[3,768,768]{2,1,0:T(8,128)(2,1)} %copy-done, bf16[2,2,96,384]{3,2,1,0:T(8,128)(2,1)S(1)} %get-tuple-element.36.rest_4_.rest_0_, ...), custom_call_target="tpu_custom_call" | custom-call | flops 1811939328 | bytes 9437184 | tf_op jit(solution)/shard_map/screen/pallas_call | solution.py:414
  82.8 1.6 collective-permute-done.18.rest_2_.refs_1_
  84.4 1.8 %collective-permute-done.19.rest_3_.refs_2_ = bf16[2,2,96,384]{3,2,1,0:T(8,128)(2,1)S(1)} collective-permute-done((bf16[2,2,96,384]{3,2,1,0:T(8,128)(2,1)S(1)}, bf16[2,2,96,384]{3,2,1,0:T(8,128)(2,1)S(1)}, u32[]{:S(2)}, u32[]{:S(2)}) %collective-permute-start.19) | collective-permute-done | bytes 294944 | tf_op jit(solution)/shard_map/ppermute | solution.py:17
  86.2 4.1 %screen.6.refs_6_.rest_4_ = f32[2,384,768]{2,1,0:T(8,128)S(1)} custom-call(s32[3]{0:T(128)S(1)} %copy-done.3, bf16[3,768,768]{2,1,0:T(8,128)(2,1)S(1)} %get-tuple-element.34.left_ref, bf16[3,768,768]{2,1,0:T(8,128)(2,1)} %copy-done, bf16[2,2,96,384]{3,2,1,0:T(8,128)(2,1)S(1)} %get-tuple-element.40.refs_7_.rest_0_, ...), custom_call_target="tpu_custom_call" | custom-call | flops 1811939328 | bytes 9437184 | tf_op jit(solution)/shard_map/screen/pallas_call | solution.py:414
  90.4 1.6 collective-permute-start.21
  92.0 1.4 collective-permute-start.20
  93.5 6.1 %screen.5 = (bf16[2,2,96,384]{3,2,1,0:T(8,128)(2,1)S(1)}, bf16[2,2,96,384]{3,2,1,0:T(8,128)(2,1)S(1)}, bf16[2,2,96,384]{3,2,1,0:T(8,128)(2,1)S(1)}, bf16[2,2,96,384]{3,2,1,0:T(8,128)(2,1)S(1)}) custom-call(s32[3]{0:T(128)S(1)} %copy-done.3, bf16[3,768,768]{2,1,0:T(8,128)(2,1)S(1)} %get-tuple-element.34.left_ref, bf16[3,768,768]{2,1,0:T(8,128)(2,1)} %copy-done, ...), custom_call_target="tpu_custom_call" | custom-call | flops 3623878656 | bytes 10616832 | tf_op jit(solution)/shard_map/screen/pallas_call | solution.py:414
  99.6 1.6 collective-permute-start.14
  101.1 1.5 collective-permute-start.15
  103.7 6.3 %collective-permute-done.20.rest_1_ = bf16[3,2,2,96,384]{4,3,2,1,0:T(8,128)(2,1)} collective-permute-done((bf16[3,2,2,96,384]{4,3,2,1,0:T(8,128)(2,1)S(1)}, bf16[3,2,2,96,384]{4,3,2,1,0:T(8,128)(2,1)}, u32[]{:S(2)}, u32[]{:S(2)}) %collective-permute-start.20) | collective-permute-done | bytes 884768 | tf_op jit(solution)/shard_map/ppermute | solution.py:23
  110.0 6.6 %screen.7 = (bf16[2,2,96,384]{3,2,1,0:T(8,128)(2,1)S(1)}, bf16[2,2,96,384]{3,2,1,0:T(8,128)(2,1)S(1)}, bf16[2,2,96,384]{3,2,1,0:T(8,128)(2,1)S(1)}, bf16[2,2,96,384]{3,2,1,0:T(8,128)(2,1)S(1)}) custom-call(s32[3]{0:T(128)S(1)} %copy-done.3, bf16[3,768,768]{2,1,0:T(8,128)(2,1)S(1)} %get-tuple-element.34.left_ref, bf16[3,768,768]{2,1,0:T(8,128)(2,1)} %copy-done, ...), custom_call_target="tpu_custom_call" | custom-call | flops 3623878656 | bytes 10616832 | tf_op jit(solution)/shard_map/screen/pallas_call | solution.py:414
  116.6 1.3 collective-permute-start.22
  117.9 1.5 collective-permute-start.23
  119.4 1.3 collective-permute-start.24
  120.7 3.4 %collective-permute-done.22.rest_9_ = bf16[2,2,96,384]{3,2,1,0:T(8,128)(2,1)S(1)} collective-permute-done((bf16[2,2,96,384]{3,2,1,0:T(8,128)(2,1)S(1)}, bf16[2,2,96,384]{3,2,1,0:T(8,128)(2,1)S(1)}, u32[]{:S(2)}, u32[]{:S(2)}) %collective-permute-start.22) | collective-permute-done | bytes 294944 | tf_op jit(solution)/shard_map/ppermute | solution.py:17
  124.1 3.9 %collective-permute-done.23.rest_10_ = bf16[2,2,96,384]{3,2,1,0:T(8,128)(2,1)S(1)} collective-permute-done((bf16[2,2,96,384]{3,2,1,0:T(8,128)(2,1)S(1)}, bf16[2,2,96,384]{3,2,1,0:T(8,128)(2,1)S(1)}, u32[]{:S(2)}, u32[]{:S(2)}) %collective-permute-start.23) | collective-permute-done | bytes 294944 | tf_op jit(solution)/shard_map/ppermute | solution.py:17
  128.0 1.8 %collective-permute-done.24.rest_11_ = bf16[2,2,96,384]{3,2,1,0:T(8,128)(2,1)S(1)} collective-permute-done((bf16[2,2,96,384]{3,2,1,0:T(8,128)(2,1)S(1)}, bf16[2,2,96,384]{3,2,1,0:T(8,128)(2,1)S(1)}, u32[]{:S(2)}, u32[]{:S(2)}) %collective-permute-start.24) | collective-permute-done | bytes 294944 | tf_op jit(solution)/shard_map/ppermute | solution.py:17
  129.9 4.6 %sigma.2 = (bf16[2,2,2,48,384]{4,3,2,1,0:T(8,128)(2,1)S(1)}, bf16[2,2,2,48,384]{4,3,2,1,0:T(8,128)(2,1)S(1)}, bf16[2,2,2,48,384]{4,3,2,1,0:T(8,128)(2,1)S(1)}, bf16[2,2,2,48,384]{4,3,2,1,0:T(8,128)(2,1)S(1)}) custom-call(s32[3]{0:T(128)S(1)} %copy-done.3, bf16[2,2,2,2,96,384]{5,4,3,2,1,0:T(8,128)(2,1)S(1)} %pack.4.rest_0_, ...), custom_call_target="tpu_custom_call" | custom-call | flops 15040512 | bytes 3538944 | tf_op jit(solution)/shard_map/sigma/pallas_call | solution.py:227
  135.1 1.7 %collective-permute-start.26 = (bf16[2,2,2,48,384]{4,3,2,1,0:T(8,128)(2,1)S(1)}, bf16[2,2,2,48,384]{4,3,2,1,0:T(8,128)(2,1)S(1)}, u32[]{:S(2)}, u32[]{:S(2)}) collective-permute-start(bf16[2,2,2,48,384]{4,3,2,1,0:T(8,128)(2,1)S(1)} %get-tuple-element.54), channel_id=1, source_target_pairs={{0,16},{4,20},{8,24},{12,28},{16,0},{20,4},{24,8},{28,12},{1,17},{... | collective-permute-start | bytes 884744 | tf_op jit(solution)/shard_map/ppermute | solution.py:17
  136.8 1.2 collective-permute-start.27
  138.0 4.6 %sigma.3 = (bf16[2,2,2,48,384]{4,3,2,1,0:T(8,128)(2,1)S(1)}, bf16[2,2,2,48,384]{4,3,2,1,0:T(8,128)(2,1)S(1)}, bf16[2,2,2,48,384]{4,3,2,1,0:T(8,128)(2,1)S(1)}, bf16[2,2,2,48,384]{4,3,2,1,0:T(8,128)(2,1)S(1)}) custom-call(s32[3]{0:T(128)S(1)} %copy-done.3, bf16[2,2,2,2,96,384]{5,4,3,2,1,0:T(8,128)(2,1)S(1)} %pack.4.rest_0_, ...), custom_call_target="tpu_custom_call" | custom-call | flops 15040512 | bytes 3538944 | tf_op jit(solution)/shard_map/sigma/pallas_call | solution.py:227
  143.2 1.7 %collective-permute-start.29 = (bf16[2,2,2,48,384]{4,3,2,1,0:T(8,128)(2,1)S(1)}, bf16[2,2,2,48,384]{4,3,2,1,0:T(8,128)(2,1)S(1)}, u32[]{:S(2)}, u32[]{:S(2)}) collective-permute-start(bf16[2,2,2,48,384]{4,3,2,1,0:T(8,128)(2,1)S(1)} %get-tuple-element.58), channel_id=1, source_target_pairs={{0,16},{4,20},{8,24},{12,28},{16,0},{20,4},{24,8},{28,12},{1,17},{... | collective-permute-start | bytes 884744 | tf_op jit(solution)/shard_map/ppermute | solution.py:17
  145.0 1.2 collective-permute-start.30
  146.2 3.9 %collective-permute-done.27.rest_3_ = bf16[2,2,2,48,384]{4,3,2,1,0:T(8,128)(2,1)S(1)} collective-permute-done((bf16[2,2,2,48,384]{4,3,2,1,0:T(8,128)(2,1)S(1)}, bf16[2,2,2,48,384]{4,3,2,1,0:T(8,128)(2,1)S(1)}, u32[]{:S(2)}, u32[]{:S(2)}) %collective-permute-start.27) | collective-permute-done | bytes 294944 | tf_op jit(solution)/shard_map/ppermute | solution.py:17
  150.3 3.7 %collective-permute-done.28.rest_5_ = bf16[2,2,2,48,384]{4,3,2,1,0:T(8,128)(2,1)S(1)} collective-permute-done((bf16[2,2,2,48,384]{4,3,2,1,0:T(8,128)(2,1)S(1)}, bf16[2,2,2,48,384]{4,3,2,1,0:T(8,128)(2,1)S(1)}, u32[]{:S(2)}, u32[]{:S(2)}) %collective-permute-start.28) | collective-permute-done | bytes 294944 | tf_op jit(solution)/shard_map/ppermute | solution.py:17
  154.1 3.5 %collective-permute-done.29.rest_6_ = bf16[2,2,2,48,384]{4,3,2,1,0:T(8,128)(2,1)S(1)} collective-permute-done((bf16[2,2,2,48,384]{4,3,2,1,0:T(8,128)(2,1)S(1)}, bf16[2,2,2,48,384]{4,3,2,1,0:T(8,128)(2,1)S(1)}, u32[]{:S(2)}, u32[]{:S(2)}) %collective-permute-start.29) | collective-permute-done | bytes 294944 | tf_op jit(solution)/shard_map/ppermute | solution.py:17
  157.9 2.0 %collective-permute-done.32.rest_9_ = bf16[4,2,2,48,384]{4,3,2,1,0:T(8,128)(2,1)S(1)} collective-permute-done((bf16[4,2,2,48,384]{4,3,2,1,0:T(8,128)(2,1)S(1)}, bf16[4,2,2,48,384]{4,3,2,1,0:T(8,128)(2,1)S(1)}, u32[]{:S(2)}, u32[]{:S(2)}) %collective-permute-start.32) | collective-permute-done | bytes 589856 | tf_op jit(solution)/shard_map/ppermute | solution.py:17
  159.8 3.8 %collect.1 = (bf16[2,1,2,384,384]{4,3,2,1,0:T(8,128)(2,1)}, bf16[2,1,2,384,384]{4,3,2,1,0:T(8,128)(2,1)}) custom-call(s32[3]{0:T(128)S(1)} %copy-done.3, bf16[2,2,2,48,384]{4,3,2,1,0:T(8,128)(2,1)S(1)} %get-tuple-element.52.rest_0_, bf16[2,2,2,48,384]{4,3,2,1,0:T(8,128)(2,1)S(1)} %collective-permute-done.25.rest_1_, ...), custom_call_target="tpu_custom_call" | custom-call | bytes 4718592 | tf_op jit(solution)/shard_map/collect/pallas_call | solution.py:466
  (53 shorter events, 7.5 us)
Async XLA Ops:
  4.5 29.1 %collective-permute-start.1 = (bf16[2,2,2,96,384]{4,3,2,1,0:T(8,128)(2,1)}, bf16[2,2,2,96,384]{4,3,2,1,0:T(8,128)(2,1)S(1)}, u32[]{:S(2)}, u32[]{:S(2)}) collective-permute-start(bf16[2,2,2,96,384]{4,3,2,1,0:T(8,128)(2,1)} %get-tuple-element.32), channel_id=1, source_target_pairs={{0,16},{4,20},{8,24},{12,28},{16,0},{20,4},{24,8},{28,12},{1,17},{... | collective-permute-start | bytes 1769480 | tf_op jit(solution)/shard_map/ppermute | solution.py:17
  7.4 26.2 %collective-permute-start.2 = (bf16[2,2,2,96,384]{4,3,2,1,0:T(8,128)(2,1)}, bf16[2,2,2,96,384]{4,3,2,1,0:T(8,128)(2,1)S(1)}, u32[]{:S(2)}, u32[]{:S(2)}) collective-permute-start(bf16[2,2,2,96,384]{4,3,2,1,0:T(8,128)(2,1)} %get-tuple-element.33), channel_id=1, source_target_pairs={{0,24},{4,28},{8,16},{12,20},{16,8},{20,12},{24,0},{28,4},{1,25},{... | collective-permute-start | bytes 1769480 | tf_op jit(solution)/shard_map/ppermute | solution.py:17
  8.9 26.0 %collective-permute-start = (bf16[2,2,2,96,384]{4,3,2,1,0:T(8,128)(2,1)}, bf16[2,2,2,96,384]{4,3,2,1,0:T(8,128)(2,1)S(1)}, u32[]{:S(2)}, u32[]{:S(2)}) collective-permute-start(bf16[2,2,2,96,384]{4,3,2,1,0:T(8,128)(2,1)} %get-tuple-element.31), channel_id=1, source_target_pairs={{0,8},{4,12},{8,0},{12,4},{16,24},{20,28},{24,16},{28,20},{1,9},{5... | collective-permute-start | bytes 1769480 | tf_op jit(solution)/shard_map/ppermute | solution.py:17
  11.5 23.4 %copy-start.1 = (bf16[2,2,2,96,384]{4,3,2,1,0:T(8,128)(2,1)S(1)}, bf16[2,2,2,96,384]{4,3,2,1,0:T(8,128)(2,1)}, u32[]{:S(2)}) copy-start(bf16[2,2,2,96,384]{4,3,2,1,0:T(8,128)(2,1)} %cut_rows.2.refs_0_) | copy-start | bytes 1769476
  33.7 4.6 %copy-start.3 = (s32[3]{0:T(128)S(1)}, s32[3]{0:T(128)}, u32[]{:S(2)}) copy-start(s32[3]{0:T(128)} %pad_add_fusion.where) | copy-start | bytes 40
  33.7 2.9 %collective-permute-start.3 = (bf16[2,2,2,2,96,384]{5,4,3,2,1,0:T(8,128)(2,1)S(1)}, bf16[2,2,2,2,96,384]{5,4,3,2,1,0:T(8,128)(2,1)S(1)}, u32[]{:S(2)}, u32[]{:S(2)}) collective-permute-start(bf16[2,2,2,2,96,384]{5,4,3,2,1,0:T(8,128)(2,1)S(1)} %pack.5.rest_1_), channel_id=1, source_target_pairs={{0,4},{4,0},{8,12},{12,8},{16,20},{20,16},{24,28},{28,24},{1,5},{5... | collective-permute-start | bytes 3538952 | tf_op jit(solution)/shard_map/ppermute | solution.py:17
  35.0 3.3 %collective-permute-start.4 = (bf16[2,2,2,2,96,384]{5,4,3,2,1,0:T(8,128)(2,1)S(1)}, bf16[2,2,2,2,96,384]{5,4,3,2,1,0:T(8,128)(2,1)S(1)}, u32[]{:S(2)}, u32[]{:S(2)}) collective-permute-start(bf16[2,2,2,2,96,384]{5,4,3,2,1,0:T(8,128)(2,1)S(1)} %pack.4.rest_0_), channel_id=1, source_target_pairs={{0,4},{4,0},{8,12},{12,8},{16,20},{20,16},{24,28},{28,24},{1,5},{5... | collective-permute-start | bytes 3538952 | tf_op jit(solution)/shard_map/ppermute | solution.py:17
  42.5 15.2 %collective-permute-start.6 = (bf16[2,2,96,384]{3,2,1,0:T(8,128)(2,1)S(1)}, bf16[2,2,96,384]{3,2,1,0:T(8,128)(2,1)S(1)}, u32[]{:S(2)}, u32[]{:S(2)}) collective-permute-start(bf16[2,2,96,384]{3,2,1,0:T(8,128)(2,1)S(1)} %get-tuple-element.37), channel_id=1, source_target_pairs={{0,8},{4,12},{8,0},{12,4},{16,24},{20,28},{24,16},{28,20},{1,9},{5... | collective-permute-start | bytes 884744 | tf_op jit(solution)/shard_map/ppermute | solution.py:17
  44.3 14.3 %collective-permute-start.7 = (bf16[2,2,96,384]{3,2,1,0:T(8,128)(2,1)S(1)}, bf16[2,2,96,384]{3,2,1,0:T(8,128)(2,1)S(1)}, u32[]{:S(2)}, u32[]{:S(2)}) collective-permute-start(bf16[2,2,96,384]{3,2,1,0:T(8,128)(2,1)S(1)} %get-tuple-element.38), channel_id=1, source_target_pairs={{0,16},{4,20},{8,24},{12,28},{16,0},{20,4},{24,8},{28,12},{1,17},{... | collective-permute-start | bytes 884744 | tf_op jit(solution)/shard_map/ppermute | solution.py:17
  45.8 15.2 %collective-permute-start.9 = (bf16[2,2,96,384]{3,2,1,0:T(8,128)(2,1)S(1)}, bf16[2,2,96,384]{3,2,1,0:T(8,128)(2,1)S(1)}, u32[]{:S(2)}, u32[]{:S(2)}) collective-permute-start(bf16[2,2,96,384]{3,2,1,0:T(8,128)(2,1)S(1)} %get-tuple-element.36.rest_4_.rest_0_), channel_id=1, source_target_pairs={{1,2},{2,1},{5,6},{6,5},{9,10},{10,9},{13,14},{14,13},{17,18},{18,... | collective-permute-start | bytes 884744 | tf_op jit(solution)/shard_map/ppermute | solution.py:23
  46.5 14.5 %collective-permute-start.5 = (bf16[2,2,96,384]{3,2,1,0:T(8,128)(2,1)S(1)}, bf16[2,2,96,384]{3,2,1,0:T(8,128)(2,1)S(1)}, u32[]{:S(2)}, u32[]{:S(2)}) collective-permute-start(bf16[2,2,96,384]{3,2,1,0:T(8,128)(2,1)S(1)} %get-tuple-element.36.rest_4_.rest_0_), channel_id=1, source_target_pairs={{0,1},{2,3},{1,0},{3,2},{4,5},{6,7},{5,4},{7,6},{8,9},{10,11},{9,8... | collective-permute-start | bytes 884744 | tf_op jit(solution)/shard_map/ppermute | solution.py:23
  50.9 10.0 %collective-permute-start.8 = (bf16[2,2,96,384]{3,2,1,0:T(8,128)(2,1)S(1)}, bf16[2,2,96,384]{3,2,1,0:T(8,128)(2,1)S(1)}, u32[]{:S(2)}, u32[]{:S(2)}) collective-permute-start(bf16[2,2,96,384]{3,2,1,0:T(8,128)(2,1)S(1)} %get-tuple-element.39), channel_id=1, source_target_pairs={{0,24},{4,28},{8,16},{12,20},{16,8},{20,12},{24,0},{28,4},{1,25},{... | collective-permute-start | bytes 884744 | tf_op jit(solution)/shard_map/ppermute | solution.py:17
  57.7 17.8 %copy-start.2 = (bf16[1,3,2,384,384]{4,3,2,1,0:T(8,128)(2,1)S(1)}, bf16[1,3,2,384,384]{4,3,2,1,0:T(8,128)(2,1)}, u32[]{:S(2)}) copy-start(bf16[1,3,2,384,384]{4,3,2,1,0:T(8,128)(2,1)} %param.5) | copy-start | bytes 5308420
  57.7 3.2 %collective-permute-start.11 = (bf16[2,2,96,384]{3,2,1,0:T(8,128)(2,1)S(1)}, bf16[2,2,96,384]{3,2,1,0:T(8,128)(2,1)S(1)}, u32[]{:S(2)}, u32[]{:S(2)}) collective-permute-start(bf16[2,2,96,384]{3,2,1,0:T(8,128)(2,1)S(1)} %get-tuple-element.40.refs_7_.rest_0_), channel_id=1, source_target_pairs={{1,2},{2,1},{5,6},{6,5},{9,10},{10,9},{13,14},{14,13},{17,18},{18,... | collective-permute-start | bytes 884744 | tf_op jit(solution)/shard_map/ppermute | solution.py:23
  58.6 7.7 %collective-permute-start.10 = (bf16[2,2,96,384]{3,2,1,0:T(8,128)(2,1)S(1)}, bf16[2,2,96,384]{3,2,1,0:T(8,128)(2,1)S(1)}, u32[]{:S(2)}, u32[]{:S(2)}) collective-permute-start(bf16[2,2,96,384]{3,2,1,0:T(8,128)(2,1)S(1)} %get-tuple-element.40.refs_7_.rest_0_), channel_id=1, source_target_pairs={{0,1},{2,3},{1,0},{3,2},{4,5},{6,7},{5,4},{7,6},{8,9},{10,11},{9,8... | collective-permute-start | bytes 884744 | tf_op jit(solution)/shard_map/ppermute | solution.py:23
  66.4 23.9 %collective-permute-start.13 = (bf16[3,2,2,96,384]{4,3,2,1,0:T(8,128)(2,1)S(1)}, bf16[3,2,2,96,384]{4,3,2,1,0:T(8,128)(2,1)S(1)}, u32[]{:S(2)}, u32[]{:S(2)}) collective-permute-start(bf16[3,2,2,96,384]{4,3,2,1,0:T(8,128)(2,1)S(1)} %pack.6), channel_id=1, source_target_pairs={{1,2},{2,1},{5,6},{6,5},{9,10},{10,9},{13,14},{14,13},{17,18},{18,... | collective-permute-start | bytes 2654216 | tf_op jit(solution)/shard_map/ppermute | solution.py:23
  67.1 23.2 %collective-permute-start.12 = (bf16[3,2,2,96,384]{4,3,2,1,0:T(8,128)(2,1)S(1)}, bf16[3,2,2,96,384]{4,3,2,1,0:T(8,128)(2,1)S(1)}, u32[]{:S(2)}, u32[]{:S(2)}) collective-permute-start(bf16[3,2,2,96,384]{4,3,2,1,0:T(8,128)(2,1)S(1)} %pack.6), channel_id=1, source_target_pairs={{0,1},{2,3},{1,0},{3,2},{4,5},{6,7},{5,4},{7,6},{8,9},{10,11},{9,8... | collective-permute-start | bytes 2654216 | tf_op jit(solution)/shard_map/ppermute | solution.py:23
  71.7 11.1 %collective-permute-start.17 = (bf16[2,2,96,384]{3,2,1,0:T(8,128)(2,1)S(1)}, bf16[2,2,96,384]{3,2,1,0:T(8,128)(2,1)S(1)}, u32[]{:S(2)}, u32[]{:S(2)}) collective-permute-start(bf16[2,2,96,384]{3,2,1,0:T(8,128)(2,1)S(1)} %get-tuple-element.45), channel_id=1, source_target_pairs={{0,8},{4,12},{8,0},{12,4},{16,24},{20,28},{24,16},{28,20},{1,9},{5... | collective-permute-start | bytes 884744 | tf_op jit(solution)/shard_map/ppermute | solution.py:17
  73.2 11.2 %collective-permute-start.18 = (bf16[2,2,96,384]{3,2,1,0:T(8,128)(2,1)S(1)}, bf16[2,2,96,384]{3,2,1,0:T(8,128)(2,1)S(1)}, u32[]{:S(2)}, u32[]{:S(2)}) collective-permute-start(bf16[2,2,96,384]{3,2,1,0:T(8,128)(2,1)S(1)} %get-tuple-element.46), channel_id=1, source_target_pairs={{0,16},{4,20},{8,24},{12,28},{16,0},{20,4},{24,8},{28,12},{1,17},{... | collective-permute-start | bytes 884744 | tf_op jit(solution)/shard_map/ppermute | solution.py:17
  74.7 11.5 %collective-permute-start.19 = (bf16[2,2,96,384]{3,2,1,0:T(8,128)(2,1)S(1)}, bf16[2,2,96,384]{3,2,1,0:T(8,128)(2,1)S(1)}, u32[]{:S(2)}, u32[]{:S(2)}) collective-permute-start(bf16[2,2,96,384]{3,2,1,0:T(8,128)(2,1)S(1)} %get-tuple-element.47), channel_id=1, source_target_pairs={{0,24},{4,28},{8,16},{12,20},{16,8},{20,12},{24,0},{28,4},{1,25},{... | collective-permute-start | bytes 884744 | tf_op jit(solution)/shard_map/ppermute | solution.py:17
  76.9 1.7 %copy-start = (bf16[3,768,768]{2,1,0:T(8,128)(2,1)}, bf16[3,768,768]{2,1,0:T(8,128)(2,1)S(1)}, u32[]{:S(2)}) copy-start(bf16[3,768,768]{2,1,0:T(8,128)(2,1)S(1)} %get-tuple-element.35.right_ref) | copy-start | bytes 10616836
  90.4 13.3 %collective-permute-start.21 = (bf16[3,2,2,96,384]{4,3,2,1,0:T(8,128)(2,1)S(1)}, bf16[3,2,2,96,384]{4,3,2,1,0:T(8,128)(2,1)}, u32[]{:S(2)}, u32[]{:S(2)}) collective-permute-start(bf16[3,2,2,96,384]{4,3,2,1,0:T(8,128)(2,1)S(1)} %pack.7), channel_id=1, source_target_pairs={{1,2},{2,1},{5,6},{6,5},{9,10},{10,9},{13,14},{14,13},{17,18},{18,... | collective-permute-start | bytes 2654216 | tf_op jit(solution)/shard_map/ppermute | solution.py:23
  92.0 17.9 %collective-permute-start.20 = (bf16[3,2,2,96,384]{4,3,2,1,0:T(8,128)(2,1)S(1)}, bf16[3,2,2,96,384]{4,3,2,1,0:T(8,128)(2,1)}, u32[]{:S(2)}, u32[]{:S(2)}) collective-permute-start(bf16[3,2,2,96,384]{4,3,2,1,0:T(8,128)(2,1)S(1)} %pack.7), channel_id=1, source_target_pairs={{0,1},{2,3},{1,0},{3,2},{4,5},{6,7},{5,4},{7,6},{8,9},{10,11},{9,8... | collective-permute-start | bytes 2654216 | tf_op jit(solution)/shard_map/ppermute | solution.py:23
  99.6 19.8 %collective-permute-start.14 = (bf16[2,2,96,384]{3,2,1,0:T(8,128)(2,1)S(1)}, bf16[2,2,96,384]{3,2,1,0:T(8,128)(2,1)S(1)}, u32[]{:S(2)}, u32[]{:S(2)}) collective-permute-start(bf16[2,2,96,384]{3,2,1,0:T(8,128)(2,1)S(1)} %get-tuple-element.42), channel_id=1, source_target_pairs={{0,8},{4,12},{8,0},{12,4},{16,24},{20,28},{24,16},{28,20},{1,9},{5... | collective-permute-start | bytes 884744 | tf_op jit(solution)/shard_map/ppermute | solution.py:17
  101.1 19.6 %collective-permute-start.15 = (bf16[2,2,96,384]{3,2,1,0:T(8,128)(2,1)S(1)}, bf16[2,2,96,384]{3,2,1,0:T(8,128)(2,1)S(1)}, u32[]{:S(2)}, u32[]{:S(2)}) collective-permute-start(bf16[2,2,96,384]{3,2,1,0:T(8,128)(2,1)S(1)} %get-tuple-element.43), channel_id=1, source_target_pairs={{0,16},{4,20},{8,24},{12,28},{16,0},{20,4},{24,8},{28,12},{1,17},{... | collective-permute-start | bytes 884744 | tf_op jit(solution)/shard_map/ppermute | solution.py:17
  102.7 18.1 %collective-permute-start.16 = (bf16[2,2,96,384]{3,2,1,0:T(8,128)(2,1)S(1)}, bf16[2,2,96,384]{3,2,1,0:T(8,128)(2,1)S(1)}, u32[]{:S(2)}, u32[]{:S(2)}) collective-permute-start(bf16[2,2,96,384]{3,2,1,0:T(8,128)(2,1)S(1)} %get-tuple-element.44), channel_id=1, source_target_pairs={{0,24},{4,28},{8,16},{12,20},{16,8},{20,12},{24,0},{28,4},{1,25},{... | collective-permute-start | bytes 884744 | tf_op jit(solution)/shard_map/ppermute | solution.py:17
  116.6 7.5 %collective-permute-start.22 = (bf16[2,2,96,384]{3,2,1,0:T(8,128)(2,1)S(1)}, bf16[2,2,96,384]{3,2,1,0:T(8,128)(2,1)S(1)}, u32[]{:S(2)}, u32[]{:S(2)}) collective-permute-start(bf16[2,2,96,384]{3,2,1,0:T(8,128)(2,1)S(1)} %get-tuple-element.49), channel_id=1, source_target_pairs={{0,8},{4,12},{8,0},{12,4},{16,24},{20,28},{24,16},{28,20},{1,9},{5... | collective-permute-start | bytes 884744 | tf_op jit(solution)/shard_map/ppermute | solution.py:17
  117.9 10.1 %collective-permute-start.23 = (bf16[2,2,96,384]{3,2,1,0:T(8,128)(2,1)S(1)}, bf16[2,2,96,384]{3,2,1,0:T(8,128)(2,1)S(1)}, u32[]{:S(2)}, u32[]{:S(2)}) collective-permute-start(bf16[2,2,96,384]{3,2,1,0:T(8,128)(2,1)S(1)} %get-tuple-element.50), channel_id=1, source_target_pairs={{0,16},{4,20},{8,24},{12,28},{16,0},{20,4},{24,8},{28,12},{1,17},{... | collective-permute-start | bytes 884744 | tf_op jit(solution)/shard_map/ppermute | solution.py:17
  119.4 10.5 %collective-permute-start.24 = (bf16[2,2,96,384]{3,2,1,0:T(8,128)(2,1)S(1)}, bf16[2,2,96,384]{3,2,1,0:T(8,128)(2,1)S(1)}, u32[]{:S(2)}, u32[]{:S(2)}) collective-permute-start(bf16[2,2,96,384]{3,2,1,0:T(8,128)(2,1)S(1)} %get-tuple-element.51), channel_id=1, source_target_pairs={{0,24},{4,28},{8,16},{12,20},{16,8},{20,12},{24,0},{28,4},{1,25},{... | collective-permute-start | bytes 884744 | tf_op jit(solution)/shard_map/ppermute | solution.py:17
  134.4 10.5 %collective-permute-start.25 = (bf16[2,2,2,48,384]{4,3,2,1,0:T(8,128)(2,1)S(1)}, bf16[2,2,2,48,384]{4,3,2,1,0:T(8,128)(2,1)S(1)}, u32[]{:S(2)}, u32[]{:S(2)}) collective-permute-start(bf16[2,2,2,48,384]{4,3,2,1,0:T(8,128)(2,1)S(1)} %get-tuple-element.53), channel_id=1, source_target_pairs={{0,8},{4,12},{8,0},{12,4},{16,24},{20,28},{24,16},{28,20},{1,9},{5... | collective-permute-start | bytes 884744 | tf_op jit(solution)/shard_map/ppermute | solution.py:17
  135.1 11.1 %collective-permute-start.26 = (bf16[2,2,2,48,384]{4,3,2,1,0:T(8,128)(2,1)S(1)}, bf16[2,2,2,48,384]{4,3,2,1,0:T(8,128)(2,1)S(1)}, u32[]{:S(2)}, u32[]{:S(2)}) collective-permute-start(bf16[2,2,2,48,384]{4,3,2,1,0:T(8,128)(2,1)S(1)} %get-tuple-element.54), channel_id=1, source_target_pairs={{0,16},{4,20},{8,24},{12,28},{16,0},{20,4},{24,8},{28,12},{1,17},{... | collective-permute-start | bytes 884744 | tf_op jit(solution)/shard_map/ppermute | solution.py:17
  136.8 13.3 %collective-permute-start.27 = (bf16[2,2,2,48,384]{4,3,2,1,0:T(8,128)(2,1)S(1)}, bf16[2,2,2,48,384]{4,3,2,1,0:T(8,128)(2,1)S(1)}, u32[]{:S(2)}, u32[]{:S(2)}) collective-permute-start(bf16[2,2,2,48,384]{4,3,2,1,0:T(8,128)(2,1)S(1)} %get-tuple-element.55), channel_id=1, source_target_pairs={{0,24},{4,28},{8,16},{12,20},{16,8},{20,12},{24,0},{28,4},{1,25},{... | collective-permute-start | bytes 884744 | tf_op jit(solution)/shard_map/ppermute | solution.py:17
  142.6 11.5 %collective-permute-start.28 = (bf16[2,2,2,48,384]{4,3,2,1,0:T(8,128)(2,1)S(1)}, bf16[2,2,2,48,384]{4,3,2,1,0:T(8,128)(2,1)S(1)}, u32[]{:S(2)}, u32[]{:S(2)}) collective-permute-start(bf16[2,2,2,48,384]{4,3,2,1,0:T(8,128)(2,1)S(1)} %get-tuple-element.57), channel_id=1, source_target_pairs={{0,8},{4,12},{8,0},{12,4},{16,24},{20,28},{24,16},{28,20},{1,9},{5... | collective-permute-start | bytes 884744 | tf_op jit(solution)/shard_map/ppermute | solution.py:17
  143.2 14.4 %collective-permute-start.29 = (bf16[2,2,2,48,384]{4,3,2,1,0:T(8,128)(2,1)S(1)}, bf16[2,2,2,48,384]{4,3,2,1,0:T(8,128)(2,1)S(1)}, u32[]{:S(2)}, u32[]{:S(2)}) collective-permute-start(bf16[2,2,2,48,384]{4,3,2,1,0:T(8,128)(2,1)S(1)} %get-tuple-element.58), channel_id=1, source_target_pairs={{0,16},{4,20},{8,24},{12,28},{16,0},{20,4},{24,8},{28,12},{1,17},{... | collective-permute-start | bytes 884744 | tf_op jit(solution)/shard_map/ppermute | solution.py:17
  145.0 12.7 %collective-permute-start.30 = (bf16[2,2,2,48,384]{4,3,2,1,0:T(8,128)(2,1)S(1)}, bf16[2,2,2,48,384]{4,3,2,1,0:T(8,128)(2,1)S(1)}, u32[]{:S(2)}, u32[]{:S(2)}) collective-permute-start(bf16[2,2,2,48,384]{4,3,2,1,0:T(8,128)(2,1)S(1)} %get-tuple-element.59), channel_id=1, source_target_pairs={{0,24},{4,28},{8,16},{12,20},{16,8},{20,12},{24,0},{28,4},{1,25},{... | collective-permute-start | bytes 884744 | tf_op jit(solution)/shard_map/ppermute | solution.py:17
  150.3 7.6 %collective-permute-start.31 = (bf16[4,2,2,48,384]{4,3,2,1,0:T(8,128)(2,1)S(1)}, bf16[4,2,2,48,384]{4,3,2,1,0:T(8,128)(2,1)S(1)}, u32[]{:S(2)}, u32[]{:S(2)}) collective-permute-start(bf16[4,2,2,48,384]{4,3,2,1,0:T(8,128)(2,1)S(1)} %pad_maximum_fusion), channel_id=1, source_target_pairs={{0,4},{4,0},{8,12},{12,8},{16,20},{20,16},{24,28},{28,24},{1,5},{5... | collective-permute-start | bytes 1769480 | tf_op jit(solution)/shard_map/ppermute | solution.py:17
  157.8 2.1 %collective-permute-start.32 = (bf16[4,2,2,48,384]{4,3,2,1,0:T(8,128)(2,1)S(1)}, bf16[4,2,2,48,384]{4,3,2,1,0:T(8,128)(2,1)S(1)}, u32[]{:S(2)}, u32[]{:S(2)}) collective-permute-start(bf16[4,2,2,48,384]{4,3,2,1,0:T(8,128)(2,1)S(1)} %pad_maximum_fusion.1), channel_id=1, source_target_pairs={{0,4},{4,0},{8,12},{12,8},{16,20},{20,16},{24,28},{28,24},{1,5},{5... | collective-permute-start | bytes 1769480 | tf_op jit(solution)/shard_map/ppermute | solution.py:17
where the time goes:
time: 164 us
  waiting for transfers between devices  63.8 us (39%)
  Pallas kernels  51.9 us (32%)
  starting transfers between devices  44.4 us (27%)
  local copies, waits for them, and re-layouts  1.88 us (1%)
    ppermute x25, waiting for transfers between devices, swap(): lax.ppermute(value, 'energy', [(i, i ^ distance) for i in range(count)])  52.1 us
    ppermute x25, starting transfers between devices, swap(): lax.ppermute(value, 'energy', [(i, i ^ distance) for i in range(count)])  27.7 us
    pallas_call x4, Pallas kernels, screen(): pl.pallas_call(functools.partial(screen_kernel, slots, each, final), name...  20.9 us
    ppermute x8, starting transfers between devices, trade(): lax.ppermute(value, 'blk', [(i, i + 1) for i in lows] + [(i + 1, i) for i...  16.7 us
    ppermute x8, waiting for transfers between devices, trade(): lax.ppermute(value, 'blk', [(i, i + 1) for i in lows] + [(i + 1, i) for i...  11.6 us
    pallas_call x2, Pallas kernels, correlate(): pl.pallas_call(functools.partial(correlate_kernel, slots, inner, chunks,...  10.5 us
    pallas_call x2, Pallas kernels, self_energy(): pl.pallas_call(functools.partial(sigma_kernel, slots, inner, chunks, len(...  9.11 us
    pallas_call x2, Pallas kernels, cut(): pl.pallas_call(functools.partial(cut_kernel, count), name='cut_rows', out...  5.81 us
  transfers between devices with their start and end apart: 33, of which 15 were waited for; matrix products, arithmetic and copies ran while one was open for 0% of the time, Pallas kernels for 22%

commit v1 on v0

--- a/solution.py
+++ b/solution.py
@@ -144,7 +144,7 @@
                 pltpu.VMEM((total // chunks, 2, block, cols), f32),
             ],
         ),
-        compiler_params=pltpu.CompilerParams(vmem_limit_bytes=32 * 2**20),
+        compiler_params=pltpu.CompilerParams(vmem_limit_bytes=16 * 2**20),
         cost_estimate=vpu_cost(total, rows * cols // chunks, 4 * total * rows * cols),
     )(where, *mine, *sib[::-1], *after)
 
@@ -239,7 +239,7 @@
                 pltpu.VMEM((total, 2, block, cols), f32),
             ],
         ),
-        compiler_params=pltpu.CompilerParams(vmem_limit_bytes=32 * 2**20),
+        compiler_params=pltpu.CompilerParams(vmem_limit_bytes=16 * 2**20),
         cost_estimate=vpu_cost(total, rows * cols, 6 * total * rows * cols),
     )(where, *mine, *sib[::-1], *flat)
 
@@ -322,7 +322,7 @@
         in_specs=[pl.BlockSpec(memory_space=pltpu.SMEM), vmem],
         out_specs=[vmem, vmem],
         scratch_shapes=held,
-        compiler_params=pltpu.CompilerParams(vmem_limit_bytes=24 * 2**20),
+        compiler_params=pltpu.CompilerParams(vmem_limit_bytes=20 * 2**20),
         cost_estimate=pl.CostEstimate(flops=0, bytes_accessed=20 * coulomb.size, transcendentals=0),
     )(where, coulomb)
 
@@ -421,32 +421,34 @@
             pltpu.VMEM((count, each, 2 * m, m), hold),
             pltpu.VMEM((each, m, 2 * count * m), bf16),
         ],
-        compiler_params=pltpu.CompilerParams(vmem_limit_bytes=44 * 2**20),
+        compiler_params=pltpu.CompilerParams(vmem_limit_bytes=28 * 2**20),
         cost_estimate=pl.CostEstimate(flops=flops, bytes_accessed=moved, transcendentals=0),
     )(where, left_matrix, right_matrix, *operands)
     return found if final else found[0]
 
 
 def collect_kernel(slots, parts, where, *rest):
-    count = slots * parts
-    own, other = rest[:count], rest[count : count + parts]
-    less, great = rest[count + parts :]
+    own, other = rest[: slots * parts], rest[slots * parts : -2]
+    less, great = rest[-2:]
     core = where[1]
-    for k in range(count):
-
-        @pl.when(pl.program_id(0) == k)
-        def _(k=k):
-            h, j = divmod(k, slots)
-            mine, theirs = own[k][0], other[h][j]
-            less[:, 0] = jnp.where(core == 0, mine, theirs)
-            great[:, 0] = jnp.where(core == 0, theirs, mine)
-
-
-def collect(where, own, other, inner, m):
+    rows = own[0].shape[3]
+    for j in range(slots):
+
+        @pl.when(pl.program_id(0) == j)
+        def _(j=j):
+            for h in range(parts):
+                mine, theirs = own[h * slots + j][0], other[h][j]
+                at = slice(h * rows, (h + 1) * rows)
+                less[:, 0, :, at] = jnp.where(core == 0, mine, theirs)
+                great[:, 0, :, at] = jnp.where(core == 0, theirs, mine)
+
+
+def collect(where, own, other):
     parts, slots = len(own), len(own[0])
-    rows = m // (slots * parts)
+    _, inner, _, rows, m = own[0][0].shape
+    shape = (inner, 1, 2, m, m)
     if rows % 16:
-        target = jnp.zeros((2, inner, 1, 2, m, m), bf16)
+        target = jnp.zeros((2,) + shape, bf16)
         for h in range(parts):
             for j in range(slots):
                 pair = jnp.stack([own[h][j][0], other[h][j]])
@@ -455,25 +457,20 @@
                 target = lax.dynamic_update_slice_in_dim(target, pair, start, axis=4)
         return target[0], target[1]
     flat = [piece for pieces in own for piece in pieces]
-    vmem = [
-        pl.BlockSpec((1, inner, 2, rows, m), lambda i, s: (0, 0, 0, 0, 0)) for _ in flat
-    ] + [pl.BlockSpec((slots, inner, 2, rows, m), lambda i, s: (0, 0, 0, 0, 0)) for _ in other]
-    shape = (inner, 1, 2, m, m)
-    target = pl.BlockSpec(
-        (inner, 1, 2, rows, m),
-        lambda i, s: (0, 0, 0, (s[0] ^ lax.rem(i, slots)) * parts + lax.div(i, slots), 0),
-    )
+    specs = [pl.BlockSpec((1, inner, 2, rows, m), lambda i, s: (0, 0, 0, 0, 0))] * len(flat)
+    specs += [pl.BlockSpec((slots, inner, 2, rows, m), lambda i, s: (0, 0, 0, 0, 0))] * parts
+    target = pl.BlockSpec((inner, 1, 2, rows * parts, m), lambda i, s: (0, 0, 0, s[0] ^ i, 0))
     return pl.pallas_call(
         functools.partial(collect_kernel, slots, parts),
         name="collect",
         out_shape=[out_like(shape)] * 2,
         grid_spec=pltpu.PrefetchScalarGridSpec(
             num_scalar_prefetch=1,
-            grid=(parts * slots,),
-            in_specs=vmem,
+            grid=(slots,),
+            in_specs=specs,
             out_specs=[target] * 2,
         ),
-        compiler_params=pltpu.CompilerParams(vmem_limit_bytes=24 * 2**20),
+        compiler_params=pltpu.CompilerParams(vmem_limit_bytes=20 * 2**20),
         cost_estimate=pl.CostEstimate(
             flops=0, bytes_accessed=16 * inner * m * m, transcendentals=0
         ),
@@ -485,7 +482,7 @@
     slots = pieces // 2
     inner, _, _, m, _ = lesser_green.shape
     group = m // slots
-    parts = 2 if group % 32 == 0 else 1
+    parts = next((n for n in (3, 2) if group % (16 * n) == 0), 1)
     rows = group // parts
     chunks = 2
     index = lax.axis_index("energy")
@@ -516,7 +513,7 @@
     for c in range(chunks):
         far = pack(pol[c], after=after)
         crossed = [near[c][0], trade(far, 0), near[c][2], trade(far, 1)]
-        after = crossed[1::2] + starts
+        after = [far, starts[0]]
         found = screen(where, left, right, crossed, slots, starts[c])
         screens.append([found[0]] + [swap(found[j], 2 * j) for j in others])
 
@@ -525,7 +522,7 @@
         found = self_energy(where, mine, sib, screens, h, rows)
         own.append([found[0]] + [swap(found[j], 2 * j) for j in others])
         other.append(swap(jnp.stack([piece[1] for piece in own[h]]), 1))
-    return tuple(collect(where, own, other, inner, m))
+    return tuple(collect(where, own, other))
 
 
 def solution(mesh):

time: 164 us -> 160 us (0.976)
  Pallas kernels: 51.9 us -> 44.8 us
  starting transfers between devices: 44.4 us -> 49.7 us
  local copies, waits for them, and re-layouts: 1.88 us -> 0.15 us
    pallas_call x4, Pallas kernels: 20.9 us -> 14.5 us  [screen(): pl.pallas_call(functools.partial(screen_kernel, slots, each, final), name...]
    ppermute x25 -> x29, starting transfers between devices: 27.7 us -> 33.1 us  [swap(): lax.ppermute(value, 'energy', [(i, i ^ distance) for i in range(count)])]
    unnamed x8 -> x6, local copies, waits for them, and re-layouts: 1.75 us -> 0.01 us
    pallas_call x2 -> x3, Pallas kernels: 9.11 us -> 9.73 us  [self_energy(): pl.pallas_call(functools.partial(sigma_kernel, slots, inner, chunks, len(...]
    ppermute x25 -> x29, waiting for transfers between devices: 52.1 us -> 51.6 us  [swap(): lax.ppermute(value, 'energy', [(i, i ^ distance) for i in range(count)])]
  transfers between devices with their start and end apart: 33 -> 37, of which waited for: 15 -> 16; matrix products, arithmetic and copies ran while one was open for 0% -> 0% of each run, Pallas kernels for 22% -> 20%
where the time goes in v1:
time: 160 us
  waiting for transfers between devices  63.6 us (40%)
  starting transfers between devices  49.7 us (31%)
  Pallas kernels  44.8 us (28%)
    ppermute x29, waiting for transfers between devices, swap(): lax.ppermute(value, 'energy', [(i, i ^ distance) for i in range(count)])  51.6 us
    ppermute x29, starting transfers between devices, swap(): lax.ppermute(value, 'energy', [(i, i ^ distance) for i in range(count)])  33.1 us
    ppermute x8, starting transfers between devices, trade(): lax.ppermute(value, 'blk', [(i, i + 1) for i in lows] + [(i + 1, i) for i...  16.6 us
    pallas_call x4, Pallas kernels, screen(): pl.pallas_call(functools.partial(screen_kernel, slots, each, final), name...  14.5 us
    ppermute x8, waiting for transfers between devices, trade(): lax.ppermute(value, 'blk', [(i, i + 1) for i in lows] + [(i + 1, i) for i...  12 us
    pallas_call x2, Pallas kernels, correlate(): pl.pallas_call(functools.partial(correlate_kernel, slots, inner, chunks,...  10.5 us
    pallas_call x3, Pallas kernels, self_energy(): pl.pallas_call(functools.partial(sigma_kernel, slots, inner, chunks, len(...  9.73 us
    pallas_call x2, Pallas kernels, cut(): pl.pallas_call(functools.partial(cut_kernel, count), name='cut_rows', out...  5.8 us
  transfers between devices with their start and end apart: 37, of which 16 were waited for; matrix products, arithmetic and copies ran while one was open for 0% of the time, Pallas kernels for 20%

profile of v1, /device:TPU:0, one launch (start us, length us, event | category | flops | bytes accessed | tf_op | source)
XLA Modules:
  0.0 160.1 jit_solution(2870546004087070750)
XLA Ops:
  1.3 3.2 %cut_rows.3 = (bf16[2,2,2,96,384]{4,3,2,1,0:T(8,128)(2,1)}, bf16[2,2,2,96,384]{4,3,2,1,0:T(8,128)(2,1)}, bf16[2,2,2,96,384]{4,3,2,1,0:T(8,128)(2,1)}) custom-call(s32[3]{0:T(128)} %pad_add_fusion.where, bf16[2,1,2,384,384]{4,3,2,1,0:T(8,128)(2,1)} %rest_2_.1, bf16[2,1,2,384,384]{4,3,2,1,0:T(8,128)(2,1)} %rest_2_.1, bf16[2,1,2,384,384]{4,3,2,1,0:T(8,128)(2,1)} %rest_2_.1, ...), custom_call_target="tpu_custom_call" | custom-call | bytes 3538944 | tf_op jit(solution)/shard_map/cut_rows/pallas_call | solution.py:272
  4.5 3.0 %collective-permute-start.1 = (bf16[2,2,2,96,384]{4,3,2,1,0:T(8,128)(2,1)}, bf16[2,2,2,96,384]{4,3,2,1,0:T(8,128)(2,1)S(1)}, u32[]{:S(2)}, u32[]{:S(2)}) collective-permute-start(bf16[2,2,2,96,384]{4,3,2,1,0:T(8,128)(2,1)} %get-tuple-element.36), channel_id=1, source_target_pairs={{0,16},{4,20},{8,24},{12,28},{16,0},{20,4},{24,8},{28,12},{1,17},{... | collective-permute-start | bytes 1769480 | tf_op jit(solution)/shard_map/ppermute | solution.py:17
  7.5 1.4 collective-permute-start.2
  9.0 2.6 %cut_rows.2.refs_0_ = bf16[2,2,2,96,384]{4,3,2,1,0:T(8,128)(2,1)} custom-call(s32[3]{0:T(128)} %pad_add_fusion.where, bf16[2,1,2,384,384]{4,3,2,1,0:T(8,128)(2,1)} %rest_2_.1, bf16[2,1,2,384,384]{4,3,2,1,0:T(8,128)(2,1)} %rest_5_.1), custom_call_target="tpu_custom_call" | custom-call | bytes 1179648 | tf_op jit(solution)/shard_map/cut_rows/pallas_call | solution.py:272
  11.6 22.1 %collective-permute-done.1.refs_0_ = bf16[2,2,2,96,384]{4,3,2,1,0:T(8,128)(2,1)S(1)} collective-permute-done((bf16[2,2,2,96,384]{4,3,2,1,0:T(8,128)(2,1)}, bf16[2,2,2,96,384]{4,3,2,1,0:T(8,128)(2,1)S(1)}, u32[]{:S(2)}, u32[]{:S(2)}) %collective-permute-start.1) | collective-permute-done | bytes 589856 | tf_op jit(solution)/shard_map/ppermute | solution.py:17
  35.2 1.6 collective-permute-done.3.rest_2_
  36.7 1.7 %collective-permute-done.4.rest_3_ = bf16[2,2,2,2,96,384]{5,4,3,2,1,0:T(8,128)(2,1)S(1)} collective-permute-done((bf16[2,2,2,2,96,384]{5,4,3,2,1,0:T(8,128)(2,1)S(1)}, bf16[2,2,2,2,96,384]{5,4,3,2,1,0:T(8,128)(2,1)S(1)}, u32[]{:S(2)}, u32[]{:S(2)}) %collective-permute-start.4) | collective-permute-done | bytes 1179680 | tf_op jit(solution)/shard_map/ppermute | solution.py:17
  38.4 4.2 %correlate.2 = (bf16[2,2,96,384]{3,2,1,0:T(8,128)(2,1)S(1)}, bf16[2,2,96,384]{3,2,1,0:T(8,128)(2,1)S(1)}, bf16[2,2,96,384]{3,2,1,0:T(8,128)(2,1)S(1)}, bf16[2,2,96,384]{3,2,1,0:T(8,128)(2,1)S(1)}) custom-call(s32[3]{0:T(128)S(1)} %copy-done.2, bf16[2,2,2,2,96,384]{5,4,3,2,1,0:T(8,128)(2,1)S(1)} %pack.4.rest_0_, ...), custom_call_target="tpu_custom_call" | custom-call | flops 15040512 | bytes 4718592 | tf_op jit(solution)/shard_map/correlate/pallas_call | solution.py:132
  42.6 1.8 %collective-permute-start.6 = (bf16[2,2,96,384]{3,2,1,0:T(8,128)(2,1)S(1)}, bf16[2,2,96,384]{3,2,1,0:T(8,128)(2,1)S(1)}, u32[]{:S(2)}, u32[]{:S(2)}) collective-permute-start(bf16[2,2,96,384]{3,2,1,0:T(8,128)(2,1)S(1)} %get-tuple-element.41), channel_id=1, source_target_pairs={{0,8},{4,12},{8,0},{12,4},{16,24},{20,28},{24,16},{28,20},{1,9},{5... | collective-permute-start | bytes 884744 | tf_op jit(solution)/shard_map/ppermute | solution.py:17
  44.4 1.5 collective-permute-start.7
  46.6 4.4 %collective-permute-start.5 = (bf16[2,2,96,384]{3,2,1,0:T(8,128)(2,1)S(1)}, bf16[2,2,96,384]{3,2,1,0:T(8,128)(2,1)S(1)}, u32[]{:S(2)}, u32[]{:S(2)}) collective-permute-start(bf16[2,2,96,384]{3,2,1,0:T(8,128)(2,1)S(1)} %get-tuple-element.40.rest_4_.rest_0_), channel_id=1, source_target_pairs={{0,1},{2,3},{1,0},{3,2},{4,5},{6,7},{5,4},{7,6},{8,9},{10,11},{9,8... | collective-permute-start | bytes 884744 | tf_op jit(solution)/shard_map/ppermute | solution.py:23
  51.5 6.3 %correlate.3 = (bf16[2,2,96,384]{3,2,1,0:T(8,128)(2,1)S(1)}, bf16[2,2,96,384]{3,2,1,0:T(8,128)(2,1)S(1)}, bf16[2,2,96,384]{3,2,1,0:T(8,128)(2,1)S(1)}, bf16[2,2,96,384]{3,2,1,0:T(8,128)(2,1)S(1)}) custom-call(s32[3]{0:T(128)S(1)} %copy-done.2, bf16[2,2,2,2,96,384]{5,4,3,2,1,0:T(8,128)(2,1)S(1)} %pack.4.rest_0_, ...), custom_call_target="tpu_custom_call" | custom-call | flops 15040512 | bytes 4718592 | tf_op jit(solution)/shard_map/correlate/pallas_call | solution.py:132
  58.7 2.4 %collective-permute-start.10 = (bf16[2,2,96,384]{3,2,1,0:T(8,128)(2,1)S(1)}, bf16[2,2,96,384]{3,2,1,0:T(8,128)(2,1)S(1)}, u32[]{:S(2)}, u32[]{:S(2)}) collective-permute-start(bf16[2,2,96,384]{3,2,1,0:T(8,128)(2,1)S(1)} %get-tuple-element.44.refs_7_.rest_0_), channel_id=1, source_target_pairs={{0,1},{2,3},{1,0},{3,2},{4,5},{6,7},{5,4},{7,6},{8,9},{10,11},{9,8... | collective-permute-start | bytes 884744 | tf_op jit(solution)/shard_map/ppermute | solution.py:23
  61.1 5.3 %collective-permute-done.10.refs_5_.rest_0_ = bf16[2,2,96,384]{3,2,1,0:T(8,128)(2,1)S(1)} collective-permute-done((bf16[2,2,96,384]{3,2,1,0:T(8,128)(2,1)S(1)}, bf16[2,2,96,384]{3,2,1,0:T(8,128)(2,1)S(1)}, u32[]{:S(2)}, u32[]{:S(2)}) %collective-permute-start.10) | collective-permute-done | bytes 294944 | tf_op jit(solution)/shard_map/ppermute | solution.py:23
  67.2 4.6 %collective-permute-start.12 = (bf16[3,2,2,96,384]{4,3,2,1,0:T(8,128)(2,1)S(1)}, bf16[3,2,2,96,384]{4,3,2,1,0:T(8,128)(2,1)S(1)}, u32[]{:S(2)}, u32[]{:S(2)}) collective-permute-start(bf16[3,2,2,96,384]{4,3,2,1,0:T(8,128)(2,1)S(1)} %pack.6.refs_3_), channel_id=1, source_target_pairs={{0,1},{2,3},{1,0},{3,2},{4,5},{6,7},{5,4},{7,6},{8,9},{10,11},{9,8... | collective-permute-start | bytes 2654216 | tf_op jit(solution)/shard_map/ppermute | solution.py:23
  71.8 1.5 collective-permute-start.17
  73.3 1.5 collective-permute-start.18
  75.6 1.4 coupling.1
  77.0 2.6 %screen.4.rest_4_.refs_4_ = f32[2,384,768]{2,1,0:T(8,128)S(1)} custom-call(s32[3]{0:T(128)S(1)} %copy-done.2, bf16[3,768,768]{2,1,0:T(8,128)(2,1)S(1)} %get-tuple-element.38.left_ref, bf16[3,768,768]{2,1,0:T(8,128)(2,1)S(1)} %get-tuple-element.39.right_ref, bf16[2,2,96,384]{3,2,1,0:T(8,128)(2,1)S(1)} %get-tuple-element.40.rest_4_.rest_0_, ...), custom_call_target="tpu_custom_call" | custom-call | flops 1811939328 | bytes 9437184 | tf_op jit(solution)/shard_map/screen/pallas_call | solution.py:414
  79.7 1.2 collective-permute-done.17.refs_0_.rest_1_
  80.8 3.7 %collective-permute-done.18.refs_1_.rest_2_ = bf16[2,2,96,384]{3,2,1,0:T(8,128)(2,1)S(1)} collective-permute-done((bf16[2,2,96,384]{3,2,1,0:T(8,128)(2,1)S(1)}, bf16[2,2,96,384]{3,2,1,0:T(8,128)(2,1)S(1)}, u32[]{:S(2)}, u32[]{:S(2)}) %collective-permute-start.18) | collective-permute-done | bytes 294944 | tf_op jit(solution)/shard_map/ppermute | solution.py:17
  84.5 1.8 %collective-permute-done.19.refs_2_.rest_3_ = bf16[2,2,96,384]{3,2,1,0:T(8,128)(2,1)S(1)} collective-permute-done((bf16[2,2,96,384]{3,2,1,0:T(8,128)(2,1)S(1)}, bf16[2,2,96,384]{3,2,1,0:T(8,128)(2,1)S(1)}, u32[]{:S(2)}, u32[]{:S(2)}) %collective-permute-start.19) | collective-permute-done | bytes 294944 | tf_op jit(solution)/shard_map/ppermute | solution.py:17
  87.3 2.1 %collective-permute-start.20 = (bf16[3,2,2,96,384]{4,3,2,1,0:T(8,128)(2,1)S(1)}, bf16[3,2,2,96,384]{4,3,2,1,0:T(8,128)(2,1)S(1)}, u32[]{:S(2)}, u32[]{:S(2)}) collective-permute-start(bf16[3,2,2,96,384]{4,3,2,1,0:T(8,128)(2,1)S(1)} %pack.7), channel_id=1, source_target_pairs={{0,1},{2,3},{1,0},{3,2},{4,5},{6,7},{5,4},{7,6},{8,9},{10,11},{9,8... | collective-permute-start | bytes 2654216 | tf_op jit(solution)/shard_map/ppermute | solution.py:23
  89.3 2.6 %screen.6.rest_4_ = f32[2,384,768]{2,1,0:T(8,128)S(1)} custom-call(s32[3]{0:T(128)S(1)} %copy-done.2, bf16[3,768,768]{2,1,0:T(8,128)(2,1)S(1)} %get-tuple-element.38.left_ref, bf16[3,768,768]{2,1,0:T(8,128)(2,1)S(1)} %get-tuple-element.39.right_ref, bf16[2,2,96,384]{3,2,1,0:T(8,128)(2,1)S(1)} %get-tuple-element.44.refs_7_.rest_0_, ...), custom_call_target="tpu_custom_call" | custom-call | flops 1811939328 | bytes 9437184 | tf_op jit(solution)/shard_map/screen/pallas_call | solution.py:414
  92.0 4.6 %screen.5 = (bf16[2,2,96,384]{3,2,1,0:T(8,128)(2,1)S(1)}, bf16[2,2,96,384]{3,2,1,0:T(8,128)(2,1)S(1)}, bf16[2,2,96,384]{3,2,1,0:T(8,128)(2,1)S(1)}, bf16[2,2,96,384]{3,2,1,0:T(8,128)(2,1)S(1)}) custom-call(s32[3]{0:T(128)S(1)} %copy-done.2, bf16[3,768,768]{2,1,0:T(8,128)(2,1)S(1)} %get-tuple-element.38.left_ref, ...), custom_call_target="tpu_custom_call" | custom-call | flops 3623878656 | bytes 10616832 | tf_op jit(solution)/shard_map/screen/pallas_call | solution.py:414
  96.6 1.9 %collective-permute-start.14 = (bf16[2,2,96,384]{3,2,1,0:T(8,128)(2,1)S(1)}, bf16[2,2,96,384]{3,2,1,0:T(8,128)(2,1)S(1)}, u32[]{:S(2)}, u32[]{:S(2)}) collective-permute-start(bf16[2,2,96,384]{3,2,1,0:T(8,128)(2,1)S(1)} %get-tuple-element.46), channel_id=1, source_target_pairs={{0,8},{4,12},{8,0},{12,4},{16,24},{20,28},{24,16},{28,20},{1,9},{5... | collective-permute-start | bytes 884744 | tf_op jit(solution)/shard_map/ppermute | solution.py:17
  98.5 1.5 collective-permute-start.15
  100.8 6.7 %collective-permute-done.20.rest_1_ = bf16[3,2,2,96,384]{4,3,2,1,0:T(8,128)(2,1)S(1)} collective-permute-done((bf16[3,2,2,96,384]{4,3,2,1,0:T(8,128)(2,1)S(1)}, bf16[3,2,2,96,384]{4,3,2,1,0:T(8,128)(2,1)S(1)}, u32[]{:S(2)}, u32[]{:S(2)}) %collective-permute-start.20) | collective-permute-done | bytes 884768 | tf_op jit(solution)/shard_map/ppermute | solution.py:23
  107.5 4.6 %screen.7 = (bf16[2,2,96,384]{3,2,1,0:T(8,128)(2,1)S(1)}, bf16[2,2,96,384]{3,2,1,0:T(8,128)(2,1)S(1)}, bf16[2,2,96,384]{3,2,1,0:T(8,128)(2,1)S(1)}, bf16[2,2,96,384]{3,2,1,0:T(8,128)(2,1)S(1)}) custom-call(s32[3]{0:T(128)S(1)} %copy-done.2, bf16[3,768,768]{2,1,0:T(8,128)(2,1)S(1)} %get-tuple-element.38.left_ref, ...), custom_call_target="tpu_custom_call" | custom-call | flops 3623878656 | bytes 10616832 | tf_op jit(solution)/shard_map/screen/pallas_call | solution.py:414
  112.1 2.1 %collective-permute-start.22 = (bf16[2,2,96,384]{3,2,1,0:T(8,128)(2,1)S(1)}, bf16[2,2,96,384]{3,2,1,0:T(8,128)(2,1)S(1)}, u32[]{:S(2)}, u32[]{:S(2)}) collective-permute-start(bf16[2,2,96,384]{3,2,1,0:T(8,128)(2,1)S(1)} %get-tuple-element.53), channel_id=1, source_target_pairs={{0,8},{4,12},{8,0},{12,4},{16,24},{20,28},{24,16},{28,20},{1,9},{5... | collective-permute-start | bytes 884744 | tf_op jit(solution)/shard_map/ppermute | solution.py:17
  114.2 1.5 collective-permute-start.23
  116.8 5.1 %collective-permute-done.22.rest_9_ = bf16[2,2,96,384]{3,2,1,0:T(8,128)(2,1)S(1)} collective-permute-done((bf16[2,2,96,384]{3,2,1,0:T(8,128)(2,1)S(1)}, bf16[2,2,96,384]{3,2,1,0:T(8,128)(2,1)S(1)}, u32[]{:S(2)}, u32[]{:S(2)}) %collective-permute-start.22) | collective-permute-done | bytes 294944 | tf_op jit(solution)/shard_map/ppermute | solution.py:17
  121.9 3.4 %collective-permute-done.23.rest_10_ = bf16[2,2,96,384]{3,2,1,0:T(8,128)(2,1)S(1)} collective-permute-done((bf16[2,2,96,384]{3,2,1,0:T(8,128)(2,1)S(1)}, bf16[2,2,96,384]{3,2,1,0:T(8,128)(2,1)S(1)}, u32[]{:S(2)}, u32[]{:S(2)}) %collective-permute-start.23) | collective-permute-done | bytes 294944 | tf_op jit(solution)/shard_map/ppermute | solution.py:17
  125.3 1.8 %collective-permute-done.24.rest_11_ = bf16[2,2,96,384]{3,2,1,0:T(8,128)(2,1)S(1)} collective-permute-done((bf16[2,2,96,384]{3,2,1,0:T(8,128)(2,1)S(1)}, bf16[2,2,96,384]{3,2,1,0:T(8,128)(2,1)S(1)}, u32[]{:S(2)}, u32[]{:S(2)}) %collective-permute-start.24) | collective-permute-done | bytes 294944 | tf_op jit(solution)/shard_map/ppermute | solution.py:17
  127.2 3.2 %sigma.5 = (bf16[2,2,2,32,384]{4,3,2,1,0:T(8,128)(2,1)S(1)}, bf16[2,2,2,32,384]{4,3,2,1,0:T(8,128)(2,1)S(1)}, bf16[2,2,2,32,384]{4,3,2,1,0:T(8,128)(2,1)S(1)}, bf16[2,2,2,32,384]{4,3,2,1,0:T(8,128)(2,1)S(1)}) custom-call(s32[3]{0:T(128)S(1)} %copy-done.2, bf16[2,2,2,2,96,384]{5,4,3,2,1,0:T(8,128)(2,1)S(1)} %pack.4.rest_0_, ...), custom_call_target="tpu_custom_call" | custom-call | flops 10027008 | bytes 2359296 | tf_op jit(solution)/shard_map/sigma/pallas_call | solution.py:227
  131.0 1.7 %collective-permute-start.32 = (bf16[2,2,2,32,384]{4,3,2,1,0:T(8,128)(2,1)S(1)}, bf16[2,2,2,32,384]{4,3,2,1,0:T(8,128)(2,1)S(1)}, u32[]{:S(2)}, u32[]{:S(2)}) collective-permute-start(bf16[2,2,2,32,384]{4,3,2,1,0:T(8,128)(2,1)S(1)} %get-tuple-element.66), channel_id=1, source_target_pairs={{0,16},{4,20},{8,24},{12,28},{16,0},{20,4},{24,8},{28,12},{1,17},{... | collective-permute-start | bytes 589832 | tf_op jit(solution)/shard_map/ppermute | solution.py:17
  132.8 1.2 collective-permute-start.33
  134.0 3.2 %sigma.3 = (bf16[2,2,2,32,384]{4,3,2,1,0:T(8,128)(2,1)S(1)}, bf16[2,2,2,32,384]{4,3,2,1,0:T(8,128)(2,1)S(1)}, bf16[2,2,2,32,384]{4,3,2,1,0:T(8,128)(2,1)S(1)}, bf16[2,2,2,32,384]{4,3,2,1,0:T(8,128)(2,1)S(1)}) custom-call(s32[3]{0:T(128)S(1)} %copy-done.2, bf16[2,2,2,2,96,384]{5,4,3,2,1,0:T(8,128)(2,1)S(1)} %pack.4.rest_0_, ...), custom_call_target="tpu_custom_call" | custom-call | flops 10027008 | bytes 2359296 | tf_op jit(solution)/shard_map/sigma/pallas_call | solution.py:227
  137.8 1.7 %collective-permute-start.26 = (bf16[2,2,2,32,384]{4,3,2,1,0:T(8,128)(2,1)S(1)}, bf16[2,2,2,32,384]{4,3,2,1,0:T(8,128)(2,1)S(1)}, u32[]{:S(2)}, u32[]{:S(2)}) collective-permute-start(bf16[2,2,2,32,384]{4,3,2,1,0:T(8,128)(2,1)S(1)} %get-tuple-element.58), channel_id=1, source_target_pairs={{0,16},{4,20},{8,24},{12,28},{16,0},{20,4},{24,8},{28,12},{1,17},{... | collective-permute-start | bytes 589832 | tf_op jit(solution)/shard_map/ppermute | solution.py:17
  139.6 1.2 collective-permute-start.27
  140.8 3.3 %sigma.4 = (bf16[2,2,2,32,384]{4,3,2,1,0:T(8,128)(2,1)S(1)}, bf16[2,2,2,32,384]{4,3,2,1,0:T(8,128)(2,1)S(1)}, bf16[2,2,2,32,384]{4,3,2,1,0:T(8,128)(2,1)S(1)}, bf16[2,2,2,32,384]{4,3,2,1,0:T(8,128)(2,1)S(1)}) custom-call(s32[3]{0:T(128)S(1)} %copy-done.2, bf16[2,2,2,2,96,384]{5,4,3,2,1,0:T(8,128)(2,1)S(1)} %pack.4.rest_0_, ...), custom_call_target="tpu_custom_call" | custom-call | flops 10027008 | bytes 2359296 | tf_op jit(solution)/shard_map/sigma/pallas_call | solution.py:227
  144.8 1.8 %collective-permute-start.29 = (bf16[2,2,2,32,384]{4,3,2,1,0:T(8,128)(2,1)S(1)}, bf16[2,2,2,32,384]{4,3,2,1,0:T(8,128)(2,1)S(1)}, u32[]{:S(2)}, u32[]{:S(2)}) collective-permute-start(bf16[2,2,2,32,384]{4,3,2,1,0:T(8,128)(2,1)S(1)} %get-tuple-element.62), channel_id=1, source_target_pairs={{0,16},{4,20},{8,24},{12,28},{16,0},{20,4},{24,8},{28,12},{1,17},{... | collective-permute-start | bytes 589832 | tf_op jit(solution)/shard_map/ppermute | solution.py:17
  146.6 1.8 %collective-permute-start.30 = (bf16[2,2,2,32,384]{4,3,2,1,0:T(8,128)(2,1)S(1)}, bf16[2,2,2,32,384]{4,3,2,1,0:T(8,128)(2,1)S(1)}, u32[]{:S(2)}, u32[]{:S(2)}) collective-permute-start(bf16[2,2,2,32,384]{4,3,2,1,0:T(8,128)(2,1)S(1)} %get-tuple-element.63), channel_id=1, source_target_pairs={{0,24},{4,28},{8,16},{12,20},{16,8},{20,12},{24,0},{28,4},{1,25},{... | collective-permute-start | bytes 589832 | tf_op jit(solution)/shard_map/ppermute | solution.py:17
  148.5 2.2 %collective-permute-done.26.rest_2_ = bf16[2,2,2,32,384]{4,3,2,1,0:T(8,128)(2,1)S(1)} collective-permute-done((bf16[2,2,2,32,384]{4,3,2,1,0:T(8,128)(2,1)S(1)}, bf16[2,2,2,32,384]{4,3,2,1,0:T(8,128)(2,1)S(1)}, u32[]{:S(2)}, u32[]{:S(2)}) %collective-permute-start.26) | collective-permute-done | bytes 196640 | tf_op jit(solution)/shard_map/ppermute | solution.py:17
  151.3 1.7 %collective-permute-done.28.rest_5_ = bf16[2,2,2,32,384]{4,3,2,1,0:T(8,128)(2,1)S(1)} collective-permute-done((bf16[2,2,2,32,384]{4,3,2,1,0:T(8,128)(2,1)S(1)}, bf16[2,2,2,32,384]{4,3,2,1,0:T(8,128)(2,1)S(1)}, u32[]{:S(2)}, u32[]{:S(2)}) %collective-permute-start.28) | collective-permute-done | bytes 196640 | tf_op jit(solution)/shard_map/ppermute | solution.py:17
  153.1 2.6 %collective-permute-done.29.rest_6_ = bf16[2,2,2,32,384]{4,3,2,1,0:T(8,128)(2,1)S(1)} collective-permute-done((bf16[2,2,2,32,384]{4,3,2,1,0:T(8,128)(2,1)S(1)}, bf16[2,2,2,32,384]{4,3,2,1,0:T(8,128)(2,1)S(1)}, u32[]{:S(2)}, u32[]{:S(2)}) %collective-permute-start.29) | collective-permute-done | bytes 196640 | tf_op jit(solution)/shard_map/ppermute | solution.py:17
  155.9 1.7 %collective-permute-done.35.rest_13_ = bf16[4,2,2,32,384]{4,3,2,1,0:T(8,128)(2,1)S(1)} collective-permute-done((bf16[4,2,2,32,384]{4,3,2,1,0:T(8,128)(2,1)S(1)}, bf16[4,2,2,32,384]{4,3,2,1,0:T(8,128)(2,1)S(1)}, u32[]{:S(2)}, u32[]{:S(2)}) %collective-permute-start.35) | collective-permute-done | bytes 393248 | tf_op jit(solution)/shard_map/ppermute | solution.py:17
  157.6 2.5 %collect.1 = (bf16[2,1,2,384,384]{4,3,2,1,0:T(8,128)(2,1)}, bf16[2,1,2,384,384]{4,3,2,1,0:T(8,128)(2,1)}) custom-call(s32[3]{0:T(128)S(1)} %copy-done.2, bf16[2,2,2,32,384]{4,3,2,1,0:T(8,128)(2,1)S(1)} %get-tuple-element.56.rest_0_, bf16[2,2,2,32,384]{4,3,2,1,0:T(8,128)(2,1)S(1)} %collective-permute-done.25.rest_1_, ...), custom_call_target="tpu_custom_call" | custom-call | bytes 4718592 | tf_op jit(solution)/shard_map/collect/pallas_call | solution.py:463
  (65 shorter events, 11.5 us)
Async XLA Ops:
  4.5 29.1 %collective-permute-start.1 = (bf16[2,2,2,96,384]{4,3,2,1,0:T(8,128)(2,1)}, bf16[2,2,2,96,384]{4,3,2,1,0:T(8,128)(2,1)S(1)}, u32[]{:S(2)}, u32[]{:S(2)}) collective-permute-start(bf16[2,2,2,96,384]{4,3,2,1,0:T(8,128)(2,1)} %get-tuple-element.36), channel_id=1, source_target_pairs={{0,16},{4,20},{8,24},{12,28},{16,0},{20,4},{24,8},{28,12},{1,17},{... | collective-permute-start | bytes 1769480 | tf_op jit(solution)/shard_map/ppermute | solution.py:17
  7.5 26.2 %collective-permute-start.2 = (bf16[2,2,2,96,384]{4,3,2,1,0:T(8,128)(2,1)}, bf16[2,2,2,96,384]{4,3,2,1,0:T(8,128)(2,1)S(1)}, u32[]{:S(2)}, u32[]{:S(2)}) collective-permute-start(bf16[2,2,2,96,384]{4,3,2,1,0:T(8,128)(2,1)} %get-tuple-element.37), channel_id=1, source_target_pairs={{0,24},{4,28},{8,16},{12,20},{16,8},{20,12},{24,0},{28,4},{1,25},{... | collective-permute-start | bytes 1769480 | tf_op jit(solution)/shard_map/ppermute | solution.py:17
  8.9 26.0 %collective-permute-start = (bf16[2,2,2,96,384]{4,3,2,1,0:T(8,128)(2,1)}, bf16[2,2,2,96,384]{4,3,2,1,0:T(8,128)(2,1)S(1)}, u32[]{:S(2)}, u32[]{:S(2)}) collective-permute-start(bf16[2,2,2,96,384]{4,3,2,1,0:T(8,128)(2,1)} %get-tuple-element.35), channel_id=1, source_target_pairs={{0,8},{4,12},{8,0},{12,4},{16,24},{20,28},{24,16},{28,20},{1,9},{5... | collective-permute-start | bytes 1769480 | tf_op jit(solution)/shard_map/ppermute | solution.py:17
  11.6 23.4 %copy-start = (bf16[2,2,2,96,384]{4,3,2,1,0:T(8,128)(2,1)S(1)}, bf16[2,2,2,96,384]{4,3,2,1,0:T(8,128)(2,1)}, u32[]{:S(2)}) copy-start(bf16[2,2,2,96,384]{4,3,2,1,0:T(8,128)(2,1)} %cut_rows.2.refs_0_) | copy-start | bytes 1769476
  33.8 4.6 %copy-start.2 = (s32[3]{0:T(128)S(1)}, s32[3]{0:T(128)}, u32[]{:S(2)}) copy-start(s32[3]{0:T(128)} %pad_add_fusion.where) | copy-start | bytes 40
  33.8 2.9 %collective-permute-start.3 = (bf16[2,2,2,2,96,384]{5,4,3,2,1,0:T(8,128)(2,1)S(1)}, bf16[2,2,2,2,96,384]{5,4,3,2,1,0:T(8,128)(2,1)S(1)}, u32[]{:S(2)}, u32[]{:S(2)}) collective-permute-start(bf16[2,2,2,2,96,384]{5,4,3,2,1,0:T(8,128)(2,1)S(1)} %pack.5.rest_1_), channel_id=1, source_target_pairs={{0,4},{4,0},{8,12},{12,8},{16,20},{20,16},{24,28},{28,24},{1,5},{5... | collective-permute-start | bytes 3538952 | tf_op jit(solution)/shard_map/ppermute | solution.py:17
  35.1 3.3 %collective-permute-start.4 = (bf16[2,2,2,2,96,384]{5,4,3,2,1,0:T(8,128)(2,1)S(1)}, bf16[2,2,2,2,96,384]{5,4,3,2,1,0:T(8,128)(2,1)S(1)}, u32[]{:S(2)}, u32[]{:S(2)}) collective-permute-start(bf16[2,2,2,2,96,384]{5,4,3,2,1,0:T(8,128)(2,1)S(1)} %pack.4.rest_0_), channel_id=1, source_target_pairs={{0,4},{4,0},{8,12},{12,8},{16,20},{20,16},{24,28},{28,24},{1,5},{5... | collective-permute-start | bytes 3538952 | tf_op jit(solution)/shard_map/ppermute | solution.py:17
  42.6 15.2 %collective-permute-start.6 = (bf16[2,2,96,384]{3,2,1,0:T(8,128)(2,1)S(1)}, bf16[2,2,96,384]{3,2,1,0:T(8,128)(2,1)S(1)}, u32[]{:S(2)}, u32[]{:S(2)}) collective-permute-start(bf16[2,2,96,384]{3,2,1,0:T(8,128)(2,1)S(1)} %get-tuple-element.41), channel_id=1, source_target_pairs={{0,8},{4,12},{8,0},{12,4},{16,24},{20,28},{24,16},{28,20},{1,9},{5... | collective-permute-start | bytes 884744 | tf_op jit(solution)/shard_map/ppermute | solution.py:17
  44.4 14.3 %collective-permute-start.7 = (bf16[2,2,96,384]{3,2,1,0:T(8,128)(2,1)S(1)}, bf16[2,2,96,384]{3,2,1,0:T(8,128)(2,1)S(1)}, u32[]{:S(2)}, u32[]{:S(2)}) collective-permute-start(bf16[2,2,96,384]{3,2,1,0:T(8,128)(2,1)S(1)} %get-tuple-element.42), channel_id=1, source_target_pairs={{0,16},{4,20},{8,24},{12,28},{16,0},{20,4},{24,8},{28,12},{1,17},{... | collective-permute-start | bytes 884744 | tf_op jit(solution)/shard_map/ppermute | solution.py:17
  45.9 15.2 %collective-permute-start.9 = (bf16[2,2,96,384]{3,2,1,0:T(8,128)(2,1)S(1)}, bf16[2,2,96,384]{3,2,1,0:T(8,128)(2,1)S(1)}, u32[]{:S(2)}, u32[]{:S(2)}) collective-permute-start(bf16[2,2,96,384]{3,2,1,0:T(8,128)(2,1)S(1)} %get-tuple-element.40.rest_4_.rest_0_), channel_id=1, source_target_pairs={{1,2},{2,1},{5,6},{6,5},{9,10},{10,9},{13,14},{14,13},{17,18},{18,... | collective-permute-start | bytes 884744 | tf_op jit(solution)/shard_map/ppermute | solution.py:23
  46.6 14.5 %collective-permute-start.5 = (bf16[2,2,96,384]{3,2,1,0:T(8,128)(2,1)S(1)}, bf16[2,2,96,384]{3,2,1,0:T(8,128)(2,1)S(1)}, u32[]{:S(2)}, u32[]{:S(2)}) collective-permute-start(bf16[2,2,96,384]{3,2,1,0:T(8,128)(2,1)S(1)} %get-tuple-element.40.rest_4_.rest_0_), channel_id=1, source_target_pairs={{0,1},{2,3},{1,0},{3,2},{4,5},{6,7},{5,4},{7,6},{8,9},{10,11},{9,8... | collective-permute-start | bytes 884744 | tf_op jit(solution)/shard_map/ppermute | solution.py:23
  51.0 10.0 %collective-permute-start.8 = (bf16[2,2,96,384]{3,2,1,0:T(8,128)(2,1)S(1)}, bf16[2,2,96,384]{3,2,1,0:T(8,128)(2,1)S(1)}, u32[]{:S(2)}, u32[]{:S(2)}) collective-permute-start(bf16[2,2,96,384]{3,2,1,0:T(8,128)(2,1)S(1)} %get-tuple-element.43), channel_id=1, source_target_pairs={{0,24},{4,28},{8,16},{12,20},{16,8},{20,12},{24,0},{28,4},{1,25},{... | collective-permute-start | bytes 884744 | tf_op jit(solution)/shard_map/ppermute | solution.py:17
  57.8 17.8 %copy-start.1 = (bf16[1,3,2,384,384]{4,3,2,1,0:T(8,128)(2,1)S(1)}, bf16[1,3,2,384,384]{4,3,2,1,0:T(8,128)(2,1)}, u32[]{:S(2)}) copy-start(bf16[1,3,2,384,384]{4,3,2,1,0:T(8,128)(2,1)} %param.5) | copy-start | bytes 5308420
  57.8 3.2 %collective-permute-start.11 = (bf16[2,2,96,384]{3,2,1,0:T(8,128)(2,1)S(1)}, bf16[2,2,96,384]{3,2,1,0:T(8,128)(2,1)S(1)}, u32[]{:S(2)}, u32[]{:S(2)}) collective-permute-start(bf16[2,2,96,384]{3,2,1,0:T(8,128)(2,1)S(1)} %get-tuple-element.44.refs_7_.rest_0_), channel_id=1, source_target_pairs={{1,2},{2,1},{5,6},{6,5},{9,10},{10,9},{13,14},{14,13},{17,18},{18,... | collective-permute-start | bytes 884744 | tf_op jit(solution)/shard_map/ppermute | solution.py:23
  58.7 7.7 %collective-permute-start.10 = (bf16[2,2,96,384]{3,2,1,0:T(8,128)(2,1)S(1)}, bf16[2,2,96,384]{3,2,1,0:T(8,128)(2,1)S(1)}, u32[]{:S(2)}, u32[]{:S(2)}) collective-permute-start(bf16[2,2,96,384]{3,2,1,0:T(8,128)(2,1)S(1)} %get-tuple-element.44.refs_7_.rest_0_), channel_id=1, source_target_pairs={{0,1},{2,3},{1,0},{3,2},{4,5},{6,7},{5,4},{7,6},{8,9},{10,11},{9,8... | collective-permute-start | bytes 884744 | tf_op jit(solution)/shard_map/ppermute | solution.py:23
  66.5 25.5 %collective-permute-start.13 = (bf16[3,2,2,96,384]{4,3,2,1,0:T(8,128)(2,1)S(1)}, bf16[3,2,2,96,384]{4,3,2,1,0:T(8,128)(2,1)S(1)}, u32[]{:S(2)}, u32[]{:S(2)}) collective-permute-start(bf16[3,2,2,96,384]{4,3,2,1,0:T(8,128)(2,1)S(1)} %pack.6.refs_3_), channel_id=1, source_target_pairs={{1,2},{2,1},{5,6},{6,5},{9,10},{10,9},{13,14},{14,13},{17,18},{18,... | collective-permute-start | bytes 2654216 | tf_op jit(solution)/shard_map/ppermute | solution.py:23
  67.2 24.8 %collective-permute-start.12 = (bf16[3,2,2,96,384]{4,3,2,1,0:T(8,128)(2,1)S(1)}, bf16[3,2,2,96,384]{4,3,2,1,0:T(8,128)(2,1)S(1)}, u32[]{:S(2)}, u32[]{:S(2)}) collective-permute-start(bf16[3,2,2,96,384]{4,3,2,1,0:T(8,128)(2,1)S(1)} %pack.6.refs_3_), channel_id=1, source_target_pairs={{0,1},{2,3},{1,0},{3,2},{4,5},{6,7},{5,4},{7,6},{8,9},{10,11},{9,8... | collective-permute-start | bytes 2654216 | tf_op jit(solution)/shard_map/ppermute | solution.py:23
  71.8 9.1 %collective-permute-start.17 = (bf16[2,2,96,384]{3,2,1,0:T(8,128)(2,1)S(1)}, bf16[2,2,96,384]{3,2,1,0:T(8,128)(2,1)S(1)}, u32[]{:S(2)}, u32[]{:S(2)}) collective-permute-start(bf16[2,2,96,384]{3,2,1,0:T(8,128)(2,1)S(1)} %get-tuple-element.49), channel_id=1, source_target_pairs={{0,8},{4,12},{8,0},{12,4},{16,24},{20,28},{24,16},{28,20},{1,9},{5... | collective-permute-start | bytes 884744 | tf_op jit(solution)/shard_map/ppermute | solution.py:17
  73.3 11.2 %collective-permute-start.18 = (bf16[2,2,96,384]{3,2,1,0:T(8,128)(2,1)S(1)}, bf16[2,2,96,384]{3,2,1,0:T(8,128)(2,1)S(1)}, u32[]{:S(2)}, u32[]{:S(2)}) collective-permute-start(bf16[2,2,96,384]{3,2,1,0:T(8,128)(2,1)S(1)} %get-tuple-element.50), channel_id=1, source_target_pairs={{0,16},{4,20},{8,24},{12,28},{16,0},{20,4},{24,8},{28,12},{1,17},{... | collective-permute-start | bytes 884744 | tf_op jit(solution)/shard_map/ppermute | solution.py:17
  74.8 11.5 %collective-permute-start.19 = (bf16[2,2,96,384]{3,2,1,0:T(8,128)(2,1)S(1)}, bf16[2,2,96,384]{3,2,1,0:T(8,128)(2,1)S(1)}, u32[]{:S(2)}, u32[]{:S(2)}) collective-permute-start(bf16[2,2,96,384]{3,2,1,0:T(8,128)(2,1)S(1)} %get-tuple-element.51), channel_id=1, source_target_pairs={{0,24},{4,28},{8,16},{12,20},{16,8},{20,12},{24,0},{28,4},{1,25},{... | collective-permute-start | bytes 884744 | tf_op jit(solution)/shard_map/ppermute | solution.py:17
  86.4 14.5 %collective-permute-start.21 = (bf16[3,2,2,96,384]{4,3,2,1,0:T(8,128)(2,1)S(1)}, bf16[3,2,2,96,384]{4,3,2,1,0:T(8,128)(2,1)S(1)}, u32[]{:S(2)}, u32[]{:S(2)}) collective-permute-start(bf16[3,2,2,96,384]{4,3,2,1,0:T(8,128)(2,1)S(1)} %pack.7), channel_id=1, source_target_pairs={{1,2},{2,1},{5,6},{6,5},{9,10},{10,9},{13,14},{14,13},{17,18},{18,... | collective-permute-start | bytes 2654216 | tf_op jit(solution)/shard_map/ppermute | solution.py:23
  87.3 20.2 %collective-permute-start.20 = (bf16[3,2,2,96,384]{4,3,2,1,0:T(8,128)(2,1)S(1)}, bf16[3,2,2,96,384]{4,3,2,1,0:T(8,128)(2,1)S(1)}, u32[]{:S(2)}, u32[]{:S(2)}) collective-permute-start(bf16[3,2,2,96,384]{4,3,2,1,0:T(8,128)(2,1)S(1)} %pack.7), channel_id=1, source_target_pairs={{0,1},{2,3},{1,0},{3,2},{4,5},{6,7},{5,4},{7,6},{8,9},{10,11},{9,8... | collective-permute-start | bytes 2654216 | tf_op jit(solution)/shard_map/ppermute | solution.py:23
  96.6 19.1 %collective-permute-start.14 = (bf16[2,2,96,384]{3,2,1,0:T(8,128)(2,1)S(1)}, bf16[2,2,96,384]{3,2,1,0:T(8,128)(2,1)S(1)}, u32[]{:S(2)}, u32[]{:S(2)}) collective-permute-start(bf16[2,2,96,384]{3,2,1,0:T(8,128)(2,1)S(1)} %get-tuple-element.46), channel_id=1, source_target_pairs={{0,8},{4,12},{8,0},{12,4},{16,24},{20,28},{24,16},{28,20},{1,9},{5... | collective-permute-start | bytes 884744 | tf_op jit(solution)/shard_map/ppermute | solution.py:17
  98.5 18.3 %collective-permute-start.15 = (bf16[2,2,96,384]{3,2,1,0:T(8,128)(2,1)S(1)}, bf16[2,2,96,384]{3,2,1,0:T(8,128)(2,1)S(1)}, u32[]{:S(2)}, u32[]{:S(2)}) collective-permute-start(bf16[2,2,96,384]{3,2,1,0:T(8,128)(2,1)S(1)} %get-tuple-element.47), channel_id=1, source_target_pairs={{0,16},{4,20},{8,24},{12,28},{16,0},{20,4},{24,8},{28,12},{1,17},{... | collective-permute-start | bytes 884744 | tf_op jit(solution)/shard_map/ppermute | solution.py:17
  100.0 16.8 %collective-permute-start.16 = (bf16[2,2,96,384]{3,2,1,0:T(8,128)(2,1)S(1)}, bf16[2,2,96,384]{3,2,1,0:T(8,128)(2,1)S(1)}, u32[]{:S(2)}, u32[]{:S(2)}) collective-permute-start(bf16[2,2,96,384]{3,2,1,0:T(8,128)(2,1)S(1)} %get-tuple-element.48), channel_id=1, source_target_pairs={{0,24},{4,28},{8,16},{12,20},{16,8},{20,12},{24,0},{28,4},{1,25},{... | collective-permute-start | bytes 884744 | tf_op jit(solution)/shard_map/ppermute | solution.py:17
  112.1 9.8 %collective-permute-start.22 = (bf16[2,2,96,384]{3,2,1,0:T(8,128)(2,1)S(1)}, bf16[2,2,96,384]{3,2,1,0:T(8,128)(2,1)S(1)}, u32[]{:S(2)}, u32[]{:S(2)}) collective-permute-start(bf16[2,2,96,384]{3,2,1,0:T(8,128)(2,1)S(1)} %get-tuple-element.53), channel_id=1, source_target_pairs={{0,8},{4,12},{8,0},{12,4},{16,24},{20,28},{24,16},{28,20},{1,9},{5... | collective-permute-start | bytes 884744 | tf_op jit(solution)/shard_map/ppermute | solution.py:17
  114.2 11.1 %collective-permute-start.23 = (bf16[2,2,96,384]{3,2,1,0:T(8,128)(2,1)S(1)}, bf16[2,2,96,384]{3,2,1,0:T(8,128)(2,1)S(1)}, u32[]{:S(2)}, u32[]{:S(2)}) collective-permute-start(bf16[2,2,96,384]{3,2,1,0:T(8,128)(2,1)S(1)} %get-tuple-element.54), channel_id=1, source_target_pairs={{0,16},{4,20},{8,24},{12,28},{16,0},{20,4},{24,8},{28,12},{1,17},{... | collective-permute-start | bytes 884744 | tf_op jit(solution)/shard_map/ppermute | solution.py:17
  115.8 11.4 %collective-permute-start.24 = (bf16[2,2,96,384]{3,2,1,0:T(8,128)(2,1)S(1)}, bf16[2,2,96,384]{3,2,1,0:T(8,128)(2,1)S(1)}, u32[]{:S(2)}, u32[]{:S(2)}) collective-permute-start(bf16[2,2,96,384]{3,2,1,0:T(8,128)(2,1)S(1)} %get-tuple-element.55), channel_id=1, source_target_pairs={{0,24},{4,28},{8,16},{12,20},{16,8},{20,12},{24,0},{28,4},{1,25},{... | collective-permute-start | bytes 884744 | tf_op jit(solution)/shard_map/ppermute | solution.py:17
  130.4 9.2 %collective-permute-start.31 = (bf16[2,2,2,32,384]{4,3,2,1,0:T(8,128)(2,1)S(1)}, bf16[2,2,2,32,384]{4,3,2,1,0:T(8,128)(2,1)S(1)}, u32[]{:S(2)}, u32[]{:S(2)}) collective-permute-start(bf16[2,2,2,32,384]{4,3,2,1,0:T(8,128)(2,1)S(1)} %get-tuple-element.65), channel_id=1, source_target_pairs={{0,8},{4,12},{8,0},{12,4},{16,24},{20,28},{24,16},{28,20},{1,9},{5... | collective-permute-start | bytes 589832 | tf_op jit(solution)/shard_map/ppermute | solution.py:17
  131.0 13.1 %collective-permute-start.32 = (bf16[2,2,2,32,384]{4,3,2,1,0:T(8,128)(2,1)S(1)}, bf16[2,2,2,32,384]{4,3,2,1,0:T(8,128)(2,1)S(1)}, u32[]{:S(2)}, u32[]{:S(2)}) collective-permute-start(bf16[2,2,2,32,384]{4,3,2,1,0:T(8,128)(2,1)S(1)} %get-tuple-element.66), channel_id=1, source_target_pairs={{0,16},{4,20},{8,24},{12,28},{16,0},{20,4},{24,8},{28,12},{1,17},{... | collective-permute-start | bytes 589832 | tf_op jit(solution)/shard_map/ppermute | solution.py:17
  132.8 12.0 %collective-permute-start.33 = (bf16[2,2,2,32,384]{4,3,2,1,0:T(8,128)(2,1)S(1)}, bf16[2,2,2,32,384]{4,3,2,1,0:T(8,128)(2,1)S(1)}, u32[]{:S(2)}, u32[]{:S(2)}) collective-permute-start(bf16[2,2,2,32,384]{4,3,2,1,0:T(8,128)(2,1)S(1)} %get-tuple-element.67), channel_id=1, source_target_pairs={{0,24},{4,28},{8,16},{12,20},{16,8},{20,12},{24,0},{28,4},{1,25},{... | collective-permute-start | bytes 589832 | tf_op jit(solution)/shard_map/ppermute | solution.py:17
  137.2 9.4 %collective-permute-start.25 = (bf16[2,2,2,32,384]{4,3,2,1,0:T(8,128)(2,1)S(1)}, bf16[2,2,2,32,384]{4,3,2,1,0:T(8,128)(2,1)S(1)}, u32[]{:S(2)}, u32[]{:S(2)}) collective-permute-start(bf16[2,2,2,32,384]{4,3,2,1,0:T(8,128)(2,1)S(1)} %get-tuple-element.57), channel_id=1, source_target_pairs={{0,8},{4,12},{8,0},{12,4},{16,24},{20,28},{24,16},{28,20},{1,9},{5... | collective-permute-start | bytes 589832 | tf_op jit(solution)/shard_map/ppermute | solution.py:17
  137.8 12.8 %collective-permute-start.26 = (bf16[2,2,2,32,384]{4,3,2,1,0:T(8,128)(2,1)S(1)}, bf16[2,2,2,32,384]{4,3,2,1,0:T(8,128)(2,1)S(1)}, u32[]{:S(2)}, u32[]{:S(2)}) collective-permute-start(bf16[2,2,2,32,384]{4,3,2,1,0:T(8,128)(2,1)S(1)} %get-tuple-element.58), channel_id=1, source_target_pairs={{0,16},{4,20},{8,24},{12,28},{16,0},{20,4},{24,8},{28,12},{1,17},{... | collective-permute-start | bytes 589832 | tf_op jit(solution)/shard_map/ppermute | solution.py:17
  139.6 11.1 %collective-permute-start.27 = (bf16[2,2,2,32,384]{4,3,2,1,0:T(8,128)(2,1)S(1)}, bf16[2,2,2,32,384]{4,3,2,1,0:T(8,128)(2,1)S(1)}, u32[]{:S(2)}, u32[]{:S(2)}) collective-permute-start(bf16[2,2,2,32,384]{4,3,2,1,0:T(8,128)(2,1)S(1)} %get-tuple-element.59), channel_id=1, source_target_pairs={{0,24},{4,28},{8,16},{12,20},{16,8},{20,12},{24,0},{28,4},{1,25},{... | collective-permute-start | bytes 589832 | tf_op jit(solution)/shard_map/ppermute | solution.py:17
  144.1 9.0 %collective-permute-start.28 = (bf16[2,2,2,32,384]{4,3,2,1,0:T(8,128)(2,1)S(1)}, bf16[2,2,2,32,384]{4,3,2,1,0:T(8,128)(2,1)S(1)}, u32[]{:S(2)}, u32[]{:S(2)}) collective-permute-start(bf16[2,2,2,32,384]{4,3,2,1,0:T(8,128)(2,1)S(1)} %get-tuple-element.61), channel_id=1, source_target_pairs={{0,8},{4,12},{8,0},{12,4},{16,24},{20,28},{24,16},{28,20},{1,9},{5... | collective-permute-start | bytes 589832 | tf_op jit(solution)/shard_map/ppermute | solution.py:17
  144.8 10.9 %collective-permute-start.29 = (bf16[2,2,2,32,384]{4,3,2,1,0:T(8,128)(2,1)S(1)}, bf16[2,2,2,32,384]{4,3,2,1,0:T(8,128)(2,1)S(1)}, u32[]{:S(2)}, u32[]{:S(2)}) collective-permute-start(bf16[2,2,2,32,384]{4,3,2,1,0:T(8,128)(2,1)S(1)} %get-tuple-element.62), channel_id=1, source_target_pairs={{0,16},{4,20},{8,24},{12,28},{16,0},{20,4},{24,8},{28,12},{1,17},{... | collective-permute-start | bytes 589832 | tf_op jit(solution)/shard_map/ppermute | solution.py:17
  146.6 9.1 %collective-permute-start.30 = (bf16[2,2,2,32,384]{4,3,2,1,0:T(8,128)(2,1)S(1)}, bf16[2,2,2,32,384]{4,3,2,1,0:T(8,128)(2,1)S(1)}, u32[]{:S(2)}, u32[]{:S(2)}) collective-permute-start(bf16[2,2,2,32,384]{4,3,2,1,0:T(8,128)(2,1)S(1)} %get-tuple-element.63), channel_id=1, source_target_pairs={{0,24},{4,28},{8,16},{12,20},{16,8},{20,12},{24,0},{28,4},{1,25},{... | collective-permute-start | bytes 589832 | tf_op jit(solution)/shard_map/ppermute | solution.py:17
  150.6 5.2 %collective-permute-start.36 = (bf16[4,2,2,32,384]{4,3,2,1,0:T(8,128)(2,1)S(1)}, bf16[4,2,2,32,384]{4,3,2,1,0:T(8,128)(2,1)S(1)}, u32[]{:S(2)}, u32[]{:S(2)}) collective-permute-start(bf16[4,2,2,32,384]{4,3,2,1,0:T(8,128)(2,1)S(1)} %pad_maximum_fusion.2), channel_id=1, source_target_pairs={{0,4},{4,0},{8,12},{12,8},{16,20},{20,16},{24,28},{28,24},{1,5},{5... | collective-permute-start | bytes 1179656 | tf_op jit(solution)/shard_map/ppermute | solution.py:17
  150.8 5.1 %collective-permute-start.34 = (bf16[4,2,2,32,384]{4,3,2,1,0:T(8,128)(2,1)S(1)}, bf16[4,2,2,32,384]{4,3,2,1,0:T(8,128)(2,1)S(1)}, u32[]{:S(2)}, u32[]{:S(2)}) collective-permute-start(bf16[4,2,2,32,384]{4,3,2,1,0:T(8,128)(2,1)S(1)} %pad_maximum_fusion), channel_id=1, source_target_pairs={{0,4},{4,0},{8,12},{12,8},{16,20},{20,16},{24,28},{28,24},{1,5},{5... | collective-permute-start | bytes 1179656 | tf_op jit(solution)/shard_map/ppermute | solution.py:17
  155.8 1.8 %collective-permute-start.35 = (bf16[4,2,2,32,384]{4,3,2,1,0:T(8,128)(2,1)S(1)}, bf16[4,2,2,32,384]{4,3,2,1,0:T(8,128)(2,1)S(1)}, u32[]{:S(2)}, u32[]{:S(2)}) collective-permute-start(bf16[4,2,2,32,384]{4,3,2,1,0:T(8,128)(2,1)S(1)} %pad_maximum_fusion.1), channel_id=1, source_target_pairs={{0,4},{4,0},{8,12},{12,8},{16,20},{20,16},{24,28},{28,24},{1,5},{5... | collective-permute-start | bytes 1179656 | tf_op jit(solution)/shard_map/ppermute | solution.py:17
